TPU v7x, 32 devices: a whole 2x2x4 slice. The times are simulated.
32 devices in a mesh: row: 16 (over z, y, core), blk: 2 (over x).
Axes of the slice: x: 2, y: 2, z: 4, core: 2. Of those that a mesh axis runs over, the one named last changes fastest.
Arguments:
- field: bfloat16 [2, 256, 1024, 1024], P(None, 'blk', 'row'), may hold values from -400 to 400
- gain: float32 [256], P('blk'), may hold values from 0.1 to 1.9
- w_first: bfloat16 [2, 8, 32, 32], replicated, may hold values from -1 to 1
- b_first: float32 [2, 256], replicated, may hold values from -4 to 4
- w_second: bfloat16 [2, 8, 32, 32], replicated, may hold values from -1 to 1
- b_second: float32 [2, 256], replicated, may hold values from -4 to 4
Outputs:
- mixed: bfloat16 [2, 256, 1024, 1024], P(None, 'blk', 'row')
All inputs are finite; a program needn't handle non-finite values.
Results may differ from a plain program's by a relative error of at most 0.02.
Values may be sent and summed in bfloat16 or wider, within the bound.
A program may use at most 192 MiB of HBM per device.

v0:
```python
import math

import jax
import jax.numpy as jnp
from jax import lax
from jax.sharding import PartitionSpec as P

CHANNELS = 256
BLOCKS = 8
HEIGHT = 1024
MODES_Y = 512
MODES_X = 128


EPS = 1e-05
SHRINK = 0.01


def forward_table(count):
    positions = jnp.arange(count, dtype=jnp.int32)[:, None]
    frequency = jnp.arange(MODES_X, dtype=jnp.int32)[None, :]
    radians = (positions * frequency % count).astype(jnp.float32) * (2.0 * math.pi / count)
    norm_scale = 1.0 / math.sqrt(count)
    return jnp.stack(
        [jnp.cos(radians) * norm_scale, -jnp.sin(radians) * norm_scale], axis=1
    ).astype(jnp.bfloat16)


def inverse_table(count, frequency):
    column_freq = frequency[:, None]
    positions = jnp.arange(count, dtype=jnp.int32)[None, :]
    radians = (positions * column_freq % count).astype(jnp.float32) * (2.0 * math.pi / count)
    weight_k = jnp.where(column_freq == 0, 1.0, 2.0).astype(jnp.float32) / math.sqrt(count)
    return jnp.stack([jnp.cos(radians) * weight_k, -jnp.sin(radians) * weight_k], axis=0).astype(
        jnp.bfloat16
    )


def height_matrix(positions):
    mode_index = jnp.arange(MODES_Y, dtype=jnp.int32) - MODES_Y // 2
    phase_int = mode_index[:, None] * positions[None, :] % HEIGHT
    radians = phase_int.astype(jnp.float32) * (2.0 * math.pi / HEIGHT)
    norm_scale = 1.0 / math.sqrt(HEIGHT)
    cosine = (jnp.cos(radians) * norm_scale).astype(jnp.bfloat16)
    sine_part = (jnp.sin(radians) * norm_scale).astype(jnp.bfloat16)
    upper_rows = jnp.concatenate([cosine, sine_part], axis=1)
    lower_rows = jnp.concatenate([-sine_part, cosine], axis=1)
    return jnp.concatenate([upper_rows, lower_rows], axis=0)


def block_filter(real_spec, imag_spec, first_w, first_b, second_w, second_b):

    def mix_channels(values_in, weights):
        return jnp.einsum("mbjik,jio->mbjok", values_in, weights, precision=lax.Precision.HIGHEST)

    def widen_bias(vector):
        return vector[None, None, :, :, None]

    real_hidden = jax.nn.relu(
        mix_channels(real_spec, first_w[0])
        - mix_channels(imag_spec, first_w[1])
        + widen_bias(first_b[0])
    )
    imag_hidden = jax.nn.relu(
        mix_channels(imag_spec, first_w[0])
        + mix_channels(real_spec, first_w[1])
        + widen_bias(first_b[1])
    )
    real_out = (
        mix_channels(real_hidden, second_w[0])
        - mix_channels(imag_hidden, second_w[1])
        + widen_bias(second_b[0])
    )
    imag_out = (
        mix_channels(imag_hidden, second_w[0])
        + mix_channels(real_hidden, second_w[1])
        + widen_bias(second_b[1])
    )
    stacked = jnp.stack([real_out, imag_out])
    return (stacked - jnp.clip(stacked, -SHRINK, SHRINK)).astype(jnp.bfloat16)


def local(field, gain, w_first, b_first, w_second, b_second):
    slices, channels, rows_here, img_cols = field.shape
    channel_total = float(CHANNELS)
    widened = field.astype(jnp.float32)
    average = (
        lax.psum(jnp.sum(widened, axis=1).astype(jnp.bfloat16), "blk").astype(jnp.float32)
        / channel_total
    )
    centered = widened - average[:, None]
    variance = (
        lax.psum(jnp.sum(centered * centered, axis=1).astype(jnp.bfloat16), "blk").astype(
            jnp.float32
        )
        / channel_total
    )
    normed = (
        (widened - average[:, None])
        * lax.rsqrt(variance[:, None] + EPS)
        * gain[None, :, None, None]
    ).astype(jnp.bfloat16)
    forward = forward_table(img_cols)
    rowspec = jnp.einsum(
        "bchw,wrk->rhbck", normed, forward, preferred_element_type=jnp.float32
    ).astype(jnp.bfloat16)
    block_width = w_first.shape[2]
    group_count = lax.axis_size("blk")
    columns = lax.all_to_all(rowspec, "row", split_axis=4, concat_axis=1, tiled=True)
    blocks_here = BLOCKS // group_count
    first_block = lax.axis_index("blk") * blocks_here
    weight_one = lax.dynamic_slice_in_dim(w_first, first_block, blocks_here, 1)
    weight_two = lax.dynamic_slice_in_dim(w_second, first_block, blocks_here, 1)
    bias_one = lax.dynamic_slice_in_dim(
        b_first, first_block * block_width, blocks_here * block_width, 1
    )
    bias_two = lax.dynamic_slice_in_dim(
        b_second, first_block * block_width, blocks_here * block_width, 1
    )
    owned_channels = columns.shape[3]
    kx_here = columns.shape[4]
    block_count = weight_one.shape[1]
    matrix = height_matrix(jnp.arange(HEIGHT, dtype=jnp.int32))
    spectrum = jnp.dot(matrix, columns.reshape(2 * HEIGHT, -1), preferred_element_type=jnp.float32)
    spectrum = spectrum.reshape(2, MODES_Y, slices, block_count, block_width, kx_here)
    filtered = block_filter(
        spectrum[0],
        spectrum[1],
        weight_one.astype(jnp.float32),
        bias_one.reshape(2, block_count, block_width),
        weight_two.astype(jnp.float32),
        bias_two.reshape(2, block_count, block_width),
    )
    filtered = filtered.reshape(2, MODES_Y, slices, owned_channels, kx_here)
    product = jnp.dot(
        matrix.T, filtered.reshape(2 * MODES_Y, -1), preferred_element_type=jnp.float32
    )
    full_height = product.astype(jnp.bfloat16).reshape(2, HEIGHT, slices, owned_channels, kx_here)
    colfield = lax.all_to_all(full_height, "row", split_axis=1, concat_axis=4, tiled=True)
    frequency = jnp.arange(MODES_X, dtype=jnp.int32)
    inverse = inverse_table(img_cols, frequency)
    return jnp.einsum(
        "rhbck,rkw->bchw", colfield, inverse, preferred_element_type=jnp.float32
    ).astype(jnp.bfloat16)


def solution(mesh):
    return jax.shard_map(
        local,
        mesh=mesh,
        in_specs=(P(None, "blk", "row", None), P("blk"), P(), P(), P(), P()),
        out_specs=P(None, "blk", "row", None),
        check_vma=False,
    )
```

profile of v0, /device:TPU:13, one launch (start us, length us, event | category | flops | bytes accessed | tf_op | source)
XLA Modules:
  0.0 811.3 jit_solution(9547932409645710224)
XLA Ops:
  6.5 12.1 %reduce_sum.21 = bf16[2,64,1024]{2,1,0:T(8,128)(2,1)} reduce(bf16[2,128,64,1024]{3,2,1,0:T(8,128)(2,1)} %param.6, bf16[]{:T(256)} %constant.71.clone.1), dimensions={1}, to_apply=%region_0.0 | reduce | flops 16646144 | bytes 33816576 | tf_op jit(solution)/shard_map/reduce_sum | solution.py:88
  18.7 0.0 all-reduce.3.cloned.1.call-update
  18.7 0.0 all-reduce.5.cloned.1.call-start
  18.7 23.9 %all-reduce.3.cloned.1.call-done = bf16[2,64,1024]{2,1,0:T(8,128)(2,1)} async-done(((bf16[2,64,1024]{2,1,0:T(8,128)(2,1)}), bf16[2,64,1024]{2,1,0:T(8,128)(2,1)}) %all-reduce.3.cloned.1.call-update) | async-done | bytes 262160 | tf_op jit(solution)/shard_map/psum | solution.py:88
  42.7 1.0 convert_multiply_fusion
  43.7 12.4 %multiply_reduce_fusion = bf16[2,64,1024]{2,1,0:T(8,128)(2,1)} fusion(bf16[2,128,64,1024]{3,2,1,0:T(8,128)(2,1)} %param.6, f32[2,64,1024]{2,1,0:T(8,128)S(1)} %convert_multiply_fusion), kind=kLoop, calls=%fused_computation.2 | loop fusion | flops 66977792 | bytes 34340864 | tf_op jit(solution)/shard_map/reduce_sum | solution.py:93
  56.1 0.0 all-reduce.5.cloned.1.call-update
  56.1 2.2 multiply_convert_fusion.3
  58.3 21.2 %all-reduce.5.cloned.1.call-done = bf16[2,64,1024]{2,1,0:T(8,128)(2,1)} async-done(((bf16[2,64,1024]{2,1,0:T(8,128)(2,1)}), bf16[2,64,1024]{2,1,0:T(8,128)(2,1)}) %all-reduce.5.cloned.1.call-update) | async-done | bytes 262160 | tf_op jit(solution)/shard_map/psum | solution.py:93
  79.4 1.0 add_rsqrt_fusion
  80.5 22.8 %multiply_convert_fusion = bf16[2,128,64,1024]{3,2,1,0:T(8,128)(2,1)} fusion(bf16[2,128,64,1024]{3,2,1,0:T(8,128)(2,1)} %param.6, f32[128]{0:T(128)S(1)} %copy-done.5, f32[2,64,1024]{2,1,0:T(8,128)S(1)} %add_rsqrt_fusion, f32[2,64,1024]{2,1,0:T(8,128)S(1)} %convert_multiply_fusion), kind=kLoop, calls=%fused_computation.1 | loop fusion | flops 83886080 | bytes 68157952 | tf_op jit(solution)/shard_map/convert_element_type | solution.py:102
  103.3 56.1 %convert_bitcast_fusion = bf16[2,64,2,128,128]{3,4,1,2,0:T(8,128)(2,1)} fusion(bf16[2,128,64,1024]{3,2,1,0:T(8,128)(2,1)} %multiply_convert_fusion, bf16[1024,1,128]{0,2,1:T(8,128)(2,1)S(1)} %get-tuple-element.15, bf16[1024,1,128]{0,2,1:T(8,128)(2,1)S(1)} %get-tuple-element.16), kind=kOutput, calls=%fused_computation.13 | convolution fusion | flops 8595177472 | bytes 42467328 | tf_op jit(solution)/shard_map/bchw,wrk->rhbck/dot_general | solution.py:104
  159.4 12.2 %copy.68 = bf16[2,64,2,128,128]{3,1,2,0,4:T(8,128)(2,1)} copy(bf16[2,64,2,128,128]{3,4,1,2,0:T(8,128)(2,1)} %convert_bitcast_fusion) | data formatting | bytes 16777216 | tf_op jit(solution)/shard_map/convert_element_type | solution.py:106
  171.6 7.0 all-to-all-start
  178.6 0.1 add.144
  178.7 0.1 add.149
  178.8 0.1 add.141
  178.9 0.1 add.137
  179.0 8.4 %fusion.61 = bf16[512,1024]{1,0:T(8,128)(2,1)S(1)} fusion(s32[512]{0:T(512)S(1)} %iota_add_fusion), kind=kLoop, calls=%fused_computation.81 | loop fusion | flops 9961472 | bytes 1050624 | tf_op jit(solution)/shard_map/neg | solution.py:47
  187.4 9.1 %multiply_convert_fusion.1 = (bf16[512,1024]{1,0:T(8,128)(2,1)S(1)}, bf16[512,1024]{1,0:T(8,128)(2,1)S(1)}) fusion(s32[512]{0:T(512)S(1)} %iota_add_fusion), kind=kLoop, calls=%fused_computation.44 | loop fusion | flops 9437184 | bytes 2099200 | tf_op jit(solution)/shard_map/convert_element_type | solution.py:45
  196.5 164.4 %all-to-all-done = bf16[2,64,2,128,128]{3,1,2,0,4:T(8,128)(2,1)} async-done(((bf16[2,64,2,128,128]{3,1,2,0,4:T(8,128)(2,1)}), bf16[2,64,2,128,128]{3,1,2,0,4:T(8,128)(2,1)}, u32[]{:S(2)}, u32[]{:S(2)}) %all-to-all-start) | async-done | bytes 8388640 | tf_op jit(solution)/shard_map/all_to_all | solution.py:109
  360.9 24.0 %copy.69 = bf16[2,64,2,128,16,8]{1,4,0,5,3,2:T(8,128)(2,1)} copy(bf16[2,64,2,128,16,8]{3,1,2,0,5,4:T(8,128)(2,1)} %bitcast.12) | data formatting | bytes 16777216 | tf_op jit(solution)/shard_map/all_to_all | solution.py:109
  384.9 23.5 %reshape.235 = bf16[2048,2048]{0,1:T(8,128)(2,1)} reshape(bf16[2,16,64,2,128,8]{2,1,0,5,4,3:T(8,128)(2,1)} %bitcast.112) | data formatting | bytes 16777216 | tf_op jit(solution)/shard_map/reshape | solution.py:124
  408.4 11.3 %fusion.42 = f32[1024,2048]{1,0:T(8,128)S(1)} fusion(bf16[2048,2048]{0,1:T(8,128)(2,1)} %reshape.235, bf16[512,1024]{1,0:T(8,128)(2,1)S(1)} %get-tuple-element.12, bf16[512,1024]{1,0:T(8,128)(2,1)S(1)} %fusion.61, bf16[512,1024]{1,0:T(8,128)(2,1)S(1)} %get-tuple-element.11), kind=kOutput, calls=%fused_computation.49 | convolution fusion | flops 8606711808 | bytes 19922944 | tf_op jit(solution)/shard_map/dot_general | solution.py:124
  419.6 3.9 fusion.77
  423.5 5.3 copy.70
  428.9 5.3 copy.72
  434.2 7.1 fusion.20
  441.3 4.8 fusion.22
  446.1 0.0 copy-start.4
  446.1 5.1 add_maximum_fusion
  451.3 2.6 fusion.10
  453.9 2.1 fusion.12
  456.0 5.1 add_maximum_fusion.1
  461.2 2.5 add_bitcast_fusion
  463.7 2.8 add_bitcast_fusion.1
  466.5 1.9 pad_maximum_fusion
  468.3 8.7 %copy.76 = f32[2,512,2,4,32,8]{1,0,5,4,3,2:T(2,128)S(1)} copy(f32[2,512,2,4,32,8]{1,4,5,2,3,0:T(8,128)S(1)} %pad_maximum_fusion) | data formatting | bytes 16777216 | tf_op jit(solution)/shard_map/stack | solution.py:79
  477.0 5.5 copy.99
  482.5 28.4 %convolution_convert_fusion = bf16[2048,2048]{1,0:T(8,128)(2,1)} fusion(f32[1024,2048]{0,1:T(8,128)} %bitcast.118, bf16[512,1024]{1,0:T(8,128)(2,1)S(1)} %get-tuple-element.12, bf16[512,1024]{1,0:T(8,128)(2,1)S(1)} %fusion.61, bf16[512,1024]{1,0:T(8,128)(2,1)S(1)} %get-tuple-element.11), kind=kOutput, calls=%fused_computation.14 | convolution fusion | flops 8617197568 | bytes 19922944 | tf_op jit(solution)/shard_map/dot_general | solution.py:135
  510.9 12.4 %copy.77 = bf16[2048,2048]{0,1:T(8,128)(2,1)} copy(bf16[2048,2048]{1,0:T(8,128)(2,1)} %convolution_convert_fusion) | data formatting | bytes 16777216 | tf_op jit(solution)/shard_map/convert_element_type | solution.py:138
  523.3 14.4 %reshape.236 = bf16[2,1024,2,128,8]{1,0,4,3,2:T(2,128)(2,1)} reshape(bf16[2048,2048]{0,1:T(8,128)(2,1)} %copy.77) | data formatting | bytes 16777216 | tf_op jit(solution)/shard_map/reshape | solution.py:138
  537.7 16.7 %copy.78 = bf16[2,1024,2,128,8]{3,4,2,0,1:T(8,128)(2,1)} copy(bf16[2,1024,2,128,8]{1,0,4,3,2:T(2,128)(2,1)} %reshape.236) | data formatting | bytes 16777216 | tf_op jit(solution)/shard_map/reshape | solution.py:138
  554.4 4.9 all-to-all-start.1
  559.3 2.2 multiply_convert_fusion.6
  561.6 180.1 %all-to-all-done.1 = bf16[2,1024,2,128,8]{3,4,2,0,1:T(8,128)(2,1)} async-done(((bf16[2,1024,2,128,8]{3,4,2,0,1:T(8,128)(2,1)}), bf16[2,1024,2,128,8]{3,4,2,0,1:T(8,128)(2,1)}, u32[]{:S(2)}, u32[]{:S(2)}) %all-to-all-start.1) | async-done | bytes 8388640 | tf_op jit(solution)/shard_map/all_to_all | solution.py:139
  741.7 17.0 %fusion = bf16[2,128,64,1024]{1,3,0,2:T(8,128)(2,1)} fusion(bf16[2,64,2,128,16,8]{3,5,2,0,1,4:T(8,128)(2,1)} %bitcast.38, bf16[1,128,1024]{1,2,0:T(8,128)(2,1)S(1)} %get-tuple-element.14, bf16[1,128,1024]{1,2,0:T(8,128)(2,1)S(1)} %get-tuple-element.13), kind=kOutput, calls=%fused_computation.4 | convolution fusion | flops 8607760384 | bytes 42467328 | tf_op jit(solution)/shard_map/rhbck,rkw->bchw/dot_general | solution.py:142
  758.6 45.6 %copy.82 = bf16[2,128,64,1024]{3,2,1,0:T(8,128)(2,1)} copy(bf16[2,128,64,1024]{1,3,0,2:T(8,128)(2,1)} %fusion) | data formatting | bytes 67108864 | tf_op jit(solution)/shard_map/convert_element_type | solution.py:144
  (21 shorter events, 0.1 us)
Async XLA Ops:
  6.5 427.7 %copy-start = (bf16[2,8,32,32]{3,2,1,0:T(8,128)(2,1)S(1)}, bf16[2,8,32,32]{3,2,1,0:T(8,128)(2,1)}, u32[]{:S(2)}) copy-start(bf16[2,8,32,32]{3,2,1,0:T(8,128)(2,1)} %param.8) | copy-start | bytes 98308
  6.5 36.2 %all-reduce.3.cloned.1.call-start = ((), (), s32[]{:S(2)}) async-start(), calls=%async_computation.2 | async-start | bytes 524288 | tf_op jit(solution)/shard_map/psum | solution.py:88
  18.7 60.7 %all-reduce.5.cloned.1.call-start = ((), (), s32[]{:S(2)}) async-start(), calls=%async_computation.3 | async-start | bytes 524288 | tf_op jit(solution)/shard_map/psum | solution.py:93
  43.7 36.8 %copy-start.5 = (f32[128]{0:T(128)S(1)}, f32[128]{0:T(128)}, u32[]{:S(2)}) copy-start(f32[128]{0:T(128)} %param.7) | copy-start | bytes 1540
  171.6 7.0 copy-start.6
  171.6 7.0 copy-start.7
  171.6 189.3 %all-to-all-start = ((bf16[2,64,2,128,128]{3,1,2,0,4:T(8,128)(2,1)}), bf16[2,64,2,128,128]{3,1,2,0,4:T(8,128)(2,1)}, u32[]{:S(2)}, u32[]{:S(2)}) async-start(bf16[2,64,2,128,128]{3,1,2,0,4:T(8,128)(2,1)} %copy.68), calls=%async_computation | async-start | bytes 16777216 | tf_op jit(solution)/shard_map/all_to_all | solution.py:109
  434.2 7.1 copy-start.2
  441.3 4.8 copy-start.3
  446.1 5.2 copy-start.4
  554.4 187.3 %all-to-all-start.1 = ((bf16[2,1024,2,128,8]{3,4,2,0,1:T(8,128)(2,1)}), bf16[2,1024,2,128,8]{3,4,2,0,1:T(8,128)(2,1)}, u32[]{:S(2)}, u32[]{:S(2)}) async-start(bf16[2,1024,2,128,8]{3,4,2,0,1:T(8,128)(2,1)} %copy.78), calls=%async_computation.1 | async-start | bytes 16777216 | tf_op jit(solution)/shard_map/all_to_all | solution.py:139
  758.6 45.6 %copy-start.1 = (bf16[2,8,32,32]{3,2,1,0:T(8,128)(2,1)S(1)}, bf16[2,8,32,32]{3,2,1,0:T(8,128)(2,1)}, u32[]{:S(2)}) copy-start(bf16[2,8,32,32]{3,2,1,0:T(8,128)(2,1)} %param.8) | copy-start | bytes 98308
Sparse Core Ops, SparseCore 0:
  18.8 23.8 all-reduce.2
  56.2 23.1 all-reduce.4
where the time goes:
time: 818 us; the launch traced here: 811 us
  waiting for transfers between devices  390 us (48%)
  local copies, waits for them, and re-layouts  178 us (22%)
  matrix products  145 us (18%)
  other arithmetic  73.2 us (9%)
  between operations  13.9 us (2%)
  starting transfers between devices  11.9 us (1%)
    all_to_all x1, waiting for transfers between devices, local(): lax.all_to_all(full_height, 'row', split_axis=1, concat_axis=4, tiled=True)  180 us
    all_to_all x1, waiting for transfers between devices, local(): lax.all_to_all(rowspec, 'row', split_axis=4, concat_axis=1, tiled=True)  164 us
    dot_general x1, matrix products, local(): jnp.einsum('bchw,wrk->rhbck', normed, forward, preferred_element_type=jnp...  56.1 us
    convert_element_type x1, local copies, waits for them, and re-layouts, local(): return jnp.einsum('rhbck,rkw->bchw', colfield, inverse, preferred_element...  45.6 us
    dot_general x8, matrix products, mix_channels(): jnp.einsum('mbjik,jio->mbjok', values_in, weights, precision=lax.Precisio...  32.1 us
    reshape x2, local copies, waits for them, and re-layouts, local(): product.astype(jnp.bfloat16)  31.1 us
    dot_general x1, matrix products, local(): jnp.dot(matrix.T, filtered.reshape(2 * MODES_Y, -1), preferred_element_ty...  28.4 us
    all_to_all x1, local copies, waits for them, and re-layouts, local(): lax.all_to_all(rowspec, 'row', split_axis=4, concat_axis=1, tiled=True)  24 us
  transfers between devices with their start and end apart: 4, of which 4 were waited for; matrix products, arithmetic and copies ran while one was open for 3% of the time, Pallas kernels for 0%

commit v1 on v0

--- a/solution.py
+++ b/solution.py
@@ -2,7 +2,10 @@
 
 import jax
 import jax.numpy as jnp
+import numpy as np
 from jax import lax
+from jax.experimental import pallas as pl
+from jax.experimental.pallas import tpu as pltpu
 from jax.sharding import PartitionSpec as P
 
 CHANNELS = 256
@@ -144,11 +147,357 @@
     ).astype(jnp.bfloat16)
 
 
+LANES = 128
+HALF = LANES // 2
+VMEM_BYTES = 56 * 1024 * 1024
+
+
+def column_tables(count, parts):
+    k = np.arange(MODES_X)
+    phase = (np.arange(count)[:, None] * k[None, :] % count) * (2.0 * math.pi / count)
+    scale = 1.0 / math.sqrt(count)
+    forward = np.stack([np.cos(phase), -np.sin(phase)], axis=1) * scale
+    inverse = forward * np.where(k == 0, 1.0, 2.0)
+
+    def order(table):
+        split = table.reshape(count, 2, parts, MODES_X // parts)
+        return split.transpose(0, 2, 1, 3).reshape(count, 2 * MODES_X)
+
+    return (
+        order(forward).astype(np.float32).astype(jnp.bfloat16),
+        order(inverse).T.astype(np.float32).astype(jnp.bfloat16),
+    )
+
+
+def row_table():
+    m = np.arange(MODES_Y) - MODES_Y // 2
+    phase = (m[:, None] * np.arange(HEIGHT)[None, :] % HEIGHT) * (2.0 * math.pi / HEIGHT)
+    table = np.concatenate([np.cos(phase), np.sin(phase)], axis=0) / math.sqrt(HEIGHT)
+    return table.astype(np.float32).astype(jnp.bfloat16)
+
+
+def lane_index(shape):
+    return lax.broadcasted_iota(jnp.int32, shape, len(shape) - 1)
+
+
+def turn(values, shift):
+    return pltpu.roll(values, shift, 1)
+
+
+def exchange_halves(first, second):
+    low = lane_index(first.shape) < HALF
+    return (
+        jnp.where(low, first, turn(second, HALF)),
+        jnp.where(low, turn(first, HALF), second),
+    )
+
+
+def swap_parts(values):
+    quarter = HALF // 2
+    is_real = lane_index(values.shape) % HALF < quarter
+    return jnp.where(is_real, turn(values, LANES - quarter), turn(values, quarter)), is_real
+
+
+def stats_kernel(field_ref, out_ref):
+    channels, rows, cols = field_ref.shape[1:]
+    zero = jnp.zeros((rows, cols), jnp.float32)
+
+    def add(c, total):
+        return total + field_ref[0, c].astype(jnp.float32)
+
+    mean = lax.fori_loop(0, channels, add, zero, unroll=8) * (1.0 / channels)
+
+    def add_square(c, total):
+        centered = field_ref[0, c].astype(jnp.float32) - mean
+        return total + centered * centered
+
+    out_ref[0] = mean
+    out_ref[1] = lax.fori_loop(0, channels, add_square, zero, unroll=8)
+
+
+def forward_kernel(field_ref, mine_ref, other_ref, gain_ref, table_ref, out_ref, average, inv_std, normed):
+    width, rows, cols = field_ref.shape[1:]
+    half_width = width // 2
+    group = 4
+    first = pl.program_id(0) * width
+    gap = mine_ref[0] - other_ref[0]
+    average[...] = (mine_ref[0] + other_ref[0]) * 0.5
+    variance = (mine_ref[1] + other_ref[1]) * (1.0 / CHANNELS) + gap * gap * 0.25
+    inv_std[...] = lax.rsqrt(variance + EPS)
+    step = 16
+
+    @pl.loop(0, half_width // group)
+    def _(g):
+        for side in range(2):
+            for i in range(group):
+                c = side * half_width + g * group + i
+                scale = gain_ref[first + c]
+                for r in range(0, rows, step):
+                    part = slice(r, r + step)
+                    x = field_ref[0, c, part, :].astype(jnp.float32)
+                    value = (x - average[part, :]) * inv_std[part, :] * scale
+                    at = (side * group + i) * rows + r
+                    normed[at : at + step, :] = value.astype(jnp.bfloat16)
+        y = jnp.dot(normed[...], table_ref[...], preferred_element_type=jnp.float32)
+        low, high = y[: group * rows], y[group * rows :]
+        for p in range(2):
+            lanes = slice(p * LANES, (p + 1) * LANES)
+            even, odd = exchange_halves(low[:, lanes], high[:, lanes])
+            for q, packed in ((2 * p, even), (2 * p + 1, odd)):
+                out_ref[0, q, pl.ds(g * group, group)] = packed.astype(jnp.bfloat16).reshape(
+                    group, rows, LANES
+                )
+
+
+def spectral_kernel(
+    x_ref, fwd_ref, inv_ref, w1_ref, b1_ref, w2_ref, b2_ref, out_ref, spec, repeat
+):
+    owners, pairs, rows, _ = x_ref.shape
+    width = 2 * pairs
+    half_m = MODES_Y // 2
+    tile = repeat * width
+
+    def strided(c):
+        return spec.at[pl.ds(c, half_m, stride=width), :]
+
+    @pl.loop(0, pairs // 2)
+    def _(j):
+        x = jnp.concatenate(
+            [x_ref[:, 2 * j + i].reshape(owners * rows, LANES) for i in range(2)], axis=1
+        )
+        y = jnp.dot(fwd_ref[...], x, preferred_element_type=jnp.float32)
+        for i in range(2):
+            lanes = slice(i * LANES, (i + 1) * LANES)
+            swapped, is_real = swap_parts(y[MODES_Y:, lanes])
+            s = y[:MODES_Y, lanes] + jnp.where(is_real, swapped, -swapped)
+            low, high = exchange_halves(s[:half_m], s[half_m:])
+            strided(2 * j + i)[...] = low
+            strided(2 * j + i + pairs)[...] = high
+
+    def mix(values, weights_ref, bias_ref):
+        both = jnp.concatenate([v.astype(jnp.bfloat16) for v in values], axis=1)
+        u = jnp.dot(weights_ref[0], both, preferred_element_type=jnp.float32)
+        v = jnp.dot(weights_ref[1], both, preferred_element_type=jnp.float32)
+        results = []
+        for i in range(2):
+            lanes = slice(i * LANES, (i + 1) * LANES)
+            swapped, is_real = swap_parts(v[:, lanes])
+            results.append(u[:, lanes] + jnp.where(is_real, -swapped, swapped) + bias_ref[...])
+        return results
+
+    @pl.loop(0, half_m * width // (2 * tile))
+    def _(t):
+        spots = [pl.ds(pl.multiple_of((2 * t + i) * tile, tile), tile) for i in range(2)]
+        hidden = mix([spec[at, :] for at in spots], w1_ref, b1_ref)
+        hidden = [jnp.maximum(h, 0.0) for h in hidden]
+        for at, out in zip(spots, mix(hidden, w2_ref, b2_ref)):
+            spec[at, :] = out - jnp.clip(out, -SHRINK, SHRINK)
+
+    @pl.loop(0, pairs // 2)
+    def _(j):
+        columns = []
+        for i in range(2):
+            c = 2 * j + i
+            f = jnp.concatenate(
+                exchange_halves(strided(c)[...], strided(c + pairs)[...]), axis=0
+            )
+            swapped, is_real = swap_parts(f)
+            g = jnp.where(is_real, -swapped, swapped)
+            columns.append(jnp.concatenate([f, g], axis=0).astype(jnp.bfloat16))
+        y = jnp.dot(
+            inv_ref[...], jnp.concatenate(columns, axis=1), preferred_element_type=jnp.float32
+        ).astype(jnp.bfloat16)
+        for i in range(2):
+            out_ref[:, 2 * j + i] = y[:, i * LANES : (i + 1) * LANES].reshape(owners, rows, LANES)
+
+
+def inverse_kernel(y_ref, table_ref, *refs):
+    out_ref = refs[-1]
+    pairs, rows = y_ref.shape[2:4]
+    group = 4
+
+    @pl.loop(0, pairs // group)
+    def _(g):
+        sides = ([], [])
+        for p in range(2):
+            parts = [
+                y_ref[0, 2 * p + i, pl.ds(g * group, group)]
+                .reshape(group * rows, LANES)
+                .astype(jnp.float32)
+                for i in range(2)
+            ]
+            for side, values in zip(sides, exchange_halves(*parts)):
+                side.append(values.astype(jnp.bfloat16))
+        for s, side in enumerate(sides):
+            mixed = jnp.dot(
+                jnp.concatenate(side, axis=1), table_ref[...], preferred_element_type=jnp.float32
+            )
+            out_ref[0, pl.ds(s * pairs + g * group, group)] = mixed.astype(jnp.bfloat16).reshape(
+                group, rows, mixed.shape[1]
+            )
+
+
+def params(count):
+    return pltpu.CompilerParams(
+        dimension_semantics=("arbitrary",) * count, vmem_limit_bytes=VMEM_BYTES
+    )
+
+
+def cost(flops, moved):
+    return pl.CostEstimate(flops=flops, bytes_accessed=moved, transcendentals=0)
+
+
+def local_stats(field, index):
+    _, channels, rows, cols = field.shape
+    step = 16
+    return pl.pallas_call(
+        stats_kernel,
+        grid=(rows // step,),
+        in_specs=[pl.BlockSpec((1, channels, step, cols), lambda i: (index, 0, i, 0))],
+        out_specs=pl.BlockSpec((2, step, cols), lambda i: (0, i, 0)),
+        out_shape=jax.ShapeDtypeStruct((2, rows, cols), jnp.float32),
+        compiler_params=params(1),
+        cost_estimate=cost(5 * channels * rows * cols, 2 * channels * rows * cols),
+        name="stats",
+    )(field)
+
+
+def forward_part(field, index, mine, other, gain, table, width):
+    _, channels, rows, cols = field.shape
+    blocks = channels // width
+    whole = lambda *shape: pl.BlockSpec(shape, lambda i: (0,) * len(shape))
+    return pl.pallas_call(
+        forward_kernel,
+        grid=(blocks,),
+        in_specs=[
+            pl.BlockSpec((1, width, rows, cols), lambda i: (index, i, 0, 0)),
+            whole(2, rows, cols),
+            whole(2, rows, cols),
+            pl.BlockSpec(memory_space=pltpu.SMEM),
+            whole(*table.shape),
+        ],
+        out_specs=pl.BlockSpec((1, 4, width // 2, rows, LANES), lambda i: (i, 0, 0, 0, 0)),
+        out_shape=jax.ShapeDtypeStruct((blocks, 4, width // 2, rows, LANES), jnp.bfloat16),
+        scratch_shapes=[
+            pltpu.VMEM((rows, cols), jnp.float32),
+            pltpu.VMEM((rows, cols), jnp.float32),
+            pltpu.VMEM((8 * rows, cols), jnp.bfloat16),
+        ],
+        compiler_params=params(1),
+        cost_estimate=cost(4 * MODES_X * channels * rows * cols, 3 * channels * rows * cols),
+        name="forward",
+    )(field, mine, other, gain, table)
+
+
+def spectral_part(columns, fwd, inv, weights_one, bias_one, weights_two, bias_two, repeat):
+    _, pairs, _, _ = columns.shape
+    vmem = pl.BlockSpec(memory_space=pltpu.VMEM)
+    return pl.pallas_call(
+        lambda *refs: spectral_kernel(*refs, repeat),
+        in_specs=[vmem] * 7,
+        out_specs=vmem,
+        out_shape=jax.ShapeDtypeStruct(columns.shape, columns.dtype),
+        scratch_shapes=[pltpu.VMEM((MODES_Y * pairs, LANES), jnp.float32)],
+        compiler_params=pltpu.CompilerParams(vmem_limit_bytes=VMEM_BYTES),
+        cost_estimate=cost(3 * 2 * HEIGHT * 2 * MODES_Y * pairs * LANES, 4 * columns.size),
+        name="spectral",
+    )(columns, fwd, inv, weights_one, bias_one, weights_two, bias_two)
+
+
+def inverse_part(received, index, table, shape, so_far):
+    blocks, parts, pairs, rows, _ = received.shape
+    slices, channels, _, cols = shape
+    width = 2 * pairs
+    operands, specs, aliases = [received, table], [
+        pl.BlockSpec((1, parts, pairs, rows, LANES), lambda i: (i, 0, 0, 0, 0)),
+        pl.BlockSpec(table.shape, lambda i: (0, 0)),
+    ], {}
+    if so_far is not None:
+        operands.append(so_far)
+        specs.append(pl.BlockSpec(memory_space=pl.ANY))
+        aliases = {2: 0}
+    return pl.pallas_call(
+        inverse_kernel,
+        grid=(blocks,),
+        in_specs=specs,
+        out_specs=pl.BlockSpec((1, width, rows, cols), lambda i: (index, i, 0, 0)),
+        out_shape=jax.ShapeDtypeStruct(shape, jnp.bfloat16),
+        input_output_aliases=aliases,
+        compiler_params=params(1),
+        cost_estimate=cost(4 * MODES_X * channels * rows * cols, 3 * channels * rows * cols),
+        name="inverse",
+    )(*operands)
+
+
+def local_packed(field, gain, w_first, b_first, w_second, b_second):
+    slices, channels, rows, cols = field.shape
+    width = w_first.shape[2]
+    blocks_here = channels // width
+    fwd_cols, inv_cols = (jnp.asarray(t) for t in column_tables(cols, 4))
+    table = row_table()
+    fwd_rows, inv_rows = jnp.asarray(table), jnp.asarray(np.ascontiguousarray(table.T))
+
+    block = lax.axis_index("blk") * blocks_here + lax.axis_index("row") // 4
+    repeat = 256 // width
+
+    def spread(weights):
+        here = lax.dynamic_index_in_dim(weights, block, 1, keepdims=False)
+        eye = jnp.eye(repeat, dtype=here.dtype)
+        tiled = eye[None, :, None, :, None] * jnp.swapaxes(here, 1, 2)[:, None, :, None, :]
+        return tiled.reshape(2, repeat * width, repeat * width)
+
+    def widen(bias):
+        here = lax.dynamic_slice_in_dim(bias, block * width, width, 1)
+        is_real = np.arange(LANES) % HALF < HALF // 2
+        tile = jnp.where(is_real[None, :], here[0][:, None], here[1][:, None])
+        return jnp.tile(tile, (repeat, 1))
+
+    layers = (spread(w_first), widen(b_first), spread(w_second), widen(b_second))
+    swap = [(0, 1), (1, 0)]
+    packed, others = [], []
+    for b in range(slices):
+        mine = local_stats(field, b)
+        others.append((mine, lax.ppermute(mine, "blk", swap)))
+    for b, (mine, other) in enumerate(others):
+        part = forward_part(field, b, mine, other, gain, fwd_cols, width)
+        packed.append(part.reshape((-1,) + part.shape[2:]))
+
+    def send(values):
+        return lax.all_to_all(values, "row", split_axis=0, concat_axis=0, tiled=True)
+
+    received = []
+    columns = send(packed[0])
+    for b in range(slices):
+        following = None
+        if b + 1 < slices:
+            columns, ready = lax.optimization_barrier((columns, packed[b + 1]))
+            following = send(ready)
+        filtered = spectral_part(columns, fwd_rows, inv_rows, *layers, repeat)
+        if received:
+            received[-1], filtered = lax.optimization_barrier((received[-1], filtered))
+        received.append(send(filtered))
+        columns = following
+    mixed = None
+    for b, back in enumerate(received):
+        back = back.reshape((blocks_here, 4) + back.shape[1:])
+        mixed = inverse_part(back, b, inv_cols, field.shape, mixed)
+    return mixed
+
+
+def packs(mesh, channels, width):
+    groups, owners = mesh.shape["blk"], mesh.shape["row"]
+    return groups == 2 and owners == 4 * (channels // groups // width) and HEIGHT % (16 * owners) == 0
+
+
 def solution(mesh):
-    return jax.shard_map(
-        local,
-        mesh=mesh,
-        in_specs=(P(None, "blk", "row", None), P("blk"), P(), P(), P(), P()),
-        out_specs=P(None, "blk", "row", None),
-        check_vma=False,
-    )
+    def whole(field, gain, w_first, b_first, w_second, b_second):
+        packed = packs(mesh, field.shape[1], w_first.shape[2])
+        return jax.shard_map(
+            local_packed if packed else local,
+            mesh=mesh,
+            in_specs=(P(None, "blk", "row", None), P("blk"), P(), P(), P(), P()),
+            out_specs=P(None, "blk", "row", None),
+            check_vma=False,
+        )(field, gain, w_first, b_first, w_second, b_second)
+
+    return whole

time: 818 us -> 443 us (0.54)
  local copies, waits for them, and re-layouts: 178 us -> 6.27 us
  matrix products: 145 us -> 0 us
  Pallas kernels: 0 us -> 143 us
  waiting for transfers between devices: 390 us -> 267 us
  other arithmetic: 73.2 us -> 0.93 us
  between operations: 13.9 us -> 0.15 us
  starting transfers between devices: 11.9 us -> 24.6 us
    dot_general x12 -> x0, matrix products: 145 us -> none  [the longest x1 56.1 us: local(): jnp.einsum('bchw,wrk->rhbck', normed, forward, preferred_element_type=jnp...]
    pallas_call x0 -> x8, Pallas kernels: none -> 143 us  [the longest x2 71.3 us: spectral_part(): pl.pallas_call(lambda *refs: spectral_kernel(*refs, repeat), in_specs=[vm...]
    all_to_all x2 -> x4, waiting for transfers between devices: 344 us -> 243 us  [send(): lax.all_to_all(values, 'row', split_axis=0, concat_axis=0, tiled=True)]
    convert_element_type x3 -> x0, local copies, waits for them, and re-layouts: 70.2 us -> none  [the longest x1 45.6 us: local(): return jnp.einsum('rhbck,rkw->bchw', colfield, inverse, preferred_element...]
    reshape x3 -> x0, local copies, waits for them, and re-layouts: 54.5 us -> none  [the longest x2 31.1 us: local(): product.astype(jnp.bfloat16)]
    psum x2 -> x0, waiting for transfers between devices: 45.1 us -> none  [the longest x1 23.9 us: local(): lax.psum(jnp.sum(widened, axis=1).astype(jnp.bfloat16), 'blk')]
    convert_element_type x2 -> x1, other arithmetic: 31.9 us -> 0.01 us  [spread(): eye = jnp.eye(repeat, dtype=here.dtype)]
    reduce_sum x2 -> x0, other arithmetic: 24.5 us -> none  [the longest x1 12.4 us: local(): jnp.sum(centered * centered, axis=1).astype(jnp.bfloat16)]
  transfers between devices with their start and end apart: 4 -> 6, of which waited for: 4 -> 6; matrix products, arithmetic and copies ran while one was open for 3% -> 1% of each run, Pallas kernels for 0% -> 24%
where the time goes in v1:
time: 443 us; the launch traced here: 442 us
  waiting for transfers between devices  267 us (60%)
  Pallas kernels  143 us (32%)
  starting transfers between devices  24.6 us (6%)
  local copies, waits for them, and re-layouts  6.27 us (1%)
    all_to_all x4, waiting for transfers between devices, send(): lax.all_to_all(values, 'row', split_axis=0, concat_axis=0, tiled=True)  243 us
    pallas_call x2, Pallas kernels, spectral_part(): pl.pallas_call(lambda *refs: spectral_kernel(*refs, repeat), in_specs=[vm...  71.3 us
    pallas_call x2, Pallas kernels, forward_part(): pl.pallas_call(forward_kernel, grid=(blocks,), in_specs=[pl.BlockSpec((1,...  26.4 us
    ppermute x2, waiting for transfers between devices, local_packed(): others.append((mine, lax.ppermute(mine, 'blk', swap)))  24 us
    pallas_call x2, Pallas kernels, local_stats(): pl.pallas_call(stats_kernel, grid=(rows // step,), in_specs=[pl.BlockSpec...  22.8 us
    pallas_call x2, Pallas kernels, inverse_part(): pl.pallas_call(inverse_kernel, grid=(blocks,), in_specs=specs, out_specs=...  22.4 us
    all_to_all x4, starting transfers between devices, send(): lax.all_to_all(values, 'row', split_axis=0, concat_axis=0, tiled=True)  22.1 us
  transfers between devices with their start and end apart: 6, of which 6 were waited for; matrix products, arithmetic and copies ran while one was open for 1% of the time, Pallas kernels for 24%

profile of v1, /device:TPU:13, one launch (start us, length us, event | category | flops | bytes accessed | tf_op | source)
XLA Modules:
  0.0 441.6 jit_solution(8099668897481307392)
XLA Ops:
  0.0 11.4 %stats.2.mine_ref = f32[2,64,1024]{2,1,0:T(8,128)} custom-call(bf16[2,128,64,1024]{3,2,1,0:T(8,128)(2,1)} %field_ref.7), custom_call_target="tpu_custom_call" | custom-call | flops 41943040 | bytes 16777216 | tf_op jit(solution)/shard_map/stats/pallas_call | solution.py:353
  11.4 1.2 collective-permute-start
  12.6 11.8 %collective-permute-done.other_ref = f32[2,64,1024]{2,1,0:T(8,128)S(1)} collective-permute-done((f32[2,64,1024]{2,1,0:T(8,128)}, f32[2,64,1024]{2,1,0:T(8,128)S(1)}, u32[]{:S(2)}, u32[]{:S(2)}) %collective-permute-start) | collective-permute-done | bytes 524320 | tf_op jit(solution)/shard_map/ppermute | solution.py:460
  24.4 0.0 copy-start.1
  24.4 0.8 copy-done.1
  25.2 13.2 %forward.2 = bf16[4,4,16,64,128]{4,3,2,1,0:T(8,128)(2,1)} custom-call(bf16[2,128,64,1024]{3,2,1,0:T(8,128)(2,1)} %field_ref.7, f32[2,64,1024]{2,1,0:T(8,128)} %stats.2.mine_ref, f32[2,64,1024]{2,1,0:T(8,128)} %copy-done.1, f32[128]{0:T(128)} %gain_ref.3, bf16[1024,256]{1,0:T(8,128)(2,1)} %constant.47.clone.table_ref), custom_call_target="tpu_custom_call" | custom-call | flops 4294967296 | bytes 25165824 | tf_op jit(solution)/shard_map/forward/pallas_call | solution.py:369
  38.4 7.4 %all-to-all-start = ((bf16[16,16,64,128]{3,2,1,0:T(8,128)(2,1)}), bf16[16,16,64,128]{3,2,1,0:T(8,128)(2,1)}, u32[]{:S(2)}, u32[]{:S(2)}) async-start(bf16[16,16,64,128]{3,2,1,0:T(8,128)(2,1)} %bitcast.33), calls=%async_computation | async-start | bytes 8388608 | tf_op jit(solution)/shard_map/all_to_all | solution.py:466
  45.8 11.4 %stats.3.mine_ref = f32[2,64,1024]{2,1,0:T(8,128)} custom-call(bf16[2,128,64,1024]{3,2,1,0:T(8,128)(2,1)} %field_ref.7), custom_call_target="tpu_custom_call" | custom-call | flops 41943040 | bytes 16777216 | tf_op jit(solution)/shard_map/stats/pallas_call | solution.py:353
  57.2 1.2 collective-permute-start.1
  58.4 12.2 %collective-permute-done.1.other_ref = f32[2,64,1024]{2,1,0:T(8,128)S(1)} collective-permute-done((f32[2,64,1024]{2,1,0:T(8,128)}, f32[2,64,1024]{2,1,0:T(8,128)S(1)}, u32[]{:S(2)}, u32[]{:S(2)}) %collective-permute-start.1) | collective-permute-done | bytes 524320 | tf_op jit(solution)/shard_map/ppermute | solution.py:460
  70.7 0.0 copy-start
  70.7 0.8 copy-done
  71.5 13.2 %forward.3 = bf16[4,4,16,64,128]{4,3,2,1,0:T(8,128)(2,1)} custom-call(bf16[2,128,64,1024]{3,2,1,0:T(8,128)(2,1)} %field_ref.7, f32[2,64,1024]{2,1,0:T(8,128)} %stats.3.mine_ref, f32[2,64,1024]{2,1,0:T(8,128)} %copy-done, f32[128]{0:T(128)} %gain_ref.3, bf16[1024,256]{1,0:T(8,128)(2,1)} %constant.47.clone.table_ref), custom_call_target="tpu_custom_call" | custom-call | flops 4294967296 | bytes 25165824 | tf_op jit(solution)/shard_map/forward/pallas_call | solution.py:369
  84.7 53.6 %all-to-all-done.refs_0_ = bf16[16,16,64,128]{3,2,1,0:T(8,128)(2,1)} async-done(((bf16[16,16,64,128]{3,2,1,0:T(8,128)(2,1)}), bf16[16,16,64,128]{3,2,1,0:T(8,128)(2,1)}, u32[]{:S(2)}, u32[]{:S(2)}) %all-to-all-start) | async-done | bytes 4194336 | tf_op jit(solution)/shard_map/all_to_all | solution.py:466
  138.3 4.9 %all-to-all-start.2 = ((bf16[16,16,64,128]{3,2,1,0:T(8,128)(2,1)}), bf16[16,16,64,128]{3,2,1,0:T(8,128)(2,1)}, u32[]{:S(2)}, u32[]{:S(2)}) async-start(bf16[16,16,64,128]{3,2,1,0:T(8,128)(2,1)} %bitcast.32), calls=%async_computation.2 | async-start | bytes 8388608 | tf_op jit(solution)/shard_map/all_to_all | solution.py:466
  143.2 0.0 copy-start.3
  143.2 0.0 copy-start.4
  143.2 0.0 copy-start.2
  143.2 0.7 dynamic-slice_bitcast_fusion
  144.0 0.1 copy.17
  144.1 0.1 copy.15
  144.2 0.1 mul.47
  144.3 0.4 mul.48
  144.7 0.2 mul.51
  144.9 0.7 mul.52
  145.6 0.2 mul.55
  145.8 0.7 mul.56
  146.5 0.0 copy-done.3
  146.5 0.0 copy-done.4
  146.6 0.1 constant_dynamic-slice_fusion
  146.6 0.0 copy-done.2
  146.6 0.1 broadcast_select_fusion
  146.7 0.8 broadcast_multiply_fusion
  147.6 0.7 tile.20
  148.2 0.7 tile.8
  148.9 35.6 %spectral.2 = bf16[16,16,64,128]{3,2,1,0:T(8,128)(2,1)} custom-call(bf16[16,16,64,128]{3,2,1,0:T(8,128)(2,1)} %all-to-all-done.refs_0_, bf16[1024,1024]{1,0:T(8,128)(2,1)} %constant.49.clone.refs_1_, bf16[1024,1024]{1,0:T(8,128)(2,1)} %constant.50.clone.refs_2_, bf16[2,256,256]{2,1,0:T(8,128)(2,1)} %get-tuple-element.14.refs_3_, f32[256,128]{1,0:T(8,128)} %bitcast.36, ...), custom_call_target="tpu_custom_call" | custom-call | flops 12884901888 | bytes 8388608 | tf_op jit(solution)/shard_map/spectral/pallas_call | solution.py:395
  184.5 51.1 %all-to-all-done.2.refs_0_ = bf16[16,16,64,128]{3,2,1,0:T(8,128)(2,1)} async-done(((bf16[16,16,64,128]{3,2,1,0:T(8,128)(2,1)}), bf16[16,16,64,128]{3,2,1,0:T(8,128)(2,1)}, u32[]{:S(2)}, u32[]{:S(2)}) %all-to-all-start.2) | async-done | bytes 4194336 | tf_op jit(solution)/shard_map/all_to_all | solution.py:466
  235.6 4.9 %all-to-all-start.1 = ((bf16[16,16,64,128]{3,2,1,0:T(8,128)(2,1)}), bf16[16,16,64,128]{3,2,1,0:T(8,128)(2,1)}, u32[]{:S(2)}, u32[]{:S(2)}) async-start(bf16[16,16,64,128]{3,2,1,0:T(8,128)(2,1)} %spectral.2), calls=%async_computation.1 | async-start | bytes 8388608 | tf_op jit(solution)/shard_map/all_to_all | solution.py:466
  240.6 35.7 %spectral.3 = bf16[16,16,64,128]{3,2,1,0:T(8,128)(2,1)} custom-call(bf16[16,16,64,128]{3,2,1,0:T(8,128)(2,1)} %all-to-all-done.2.refs_0_, bf16[1024,1024]{1,0:T(8,128)(2,1)} %constant.49.clone.refs_1_, bf16[1024,1024]{1,0:T(8,128)(2,1)} %constant.50.clone.refs_2_, bf16[2,256,256]{2,1,0:T(8,128)(2,1)} %get-tuple-element.14.refs_3_, f32[256,128]{1,0:T(8,128)} %bitcast.37, ...), custom_call_target="tpu_custom_call" | custom-call | flops 12884901888 | bytes 8388608 | tf_op jit(solution)/shard_map/spectral/pallas_call | solution.py:395
  276.2 56.8 %all-to-all-done.1 = bf16[16,16,64,128]{3,2,1,0:T(8,128)(2,1)} async-done(((bf16[16,16,64,128]{3,2,1,0:T(8,128)(2,1)}), bf16[16,16,64,128]{3,2,1,0:T(8,128)(2,1)}, u32[]{:S(2)}, u32[]{:S(2)}) %all-to-all-start.1) | async-done | bytes 4194336 | tf_op jit(solution)/shard_map/all_to_all | solution.py:466
  333.0 4.9 %all-to-all-start.3 = ((bf16[16,16,64,128]{3,2,1,0:T(8,128)(2,1)}), bf16[16,16,64,128]{3,2,1,0:T(8,128)(2,1)}, u32[]{:S(2)}, u32[]{:S(2)}) async-start(bf16[16,16,64,128]{3,2,1,0:T(8,128)(2,1)} %spectral.3), calls=%async_computation.3 | async-start | bytes 8388608 | tf_op jit(solution)/shard_map/all_to_all | solution.py:466
  337.9 11.2 %inverse.2.refs_0_ = bf16[2,128,64,1024]{3,2,1,0:T(8,128)(2,1)} custom-call(bf16[4,4,16,64,128]{4,3,2,1,0:T(8,128)(2,1)} %bitcast.13.y_ref, bf16[256,1024]{1,0:T(8,128)(2,1)} %constant.48.clone.table_ref), custom_call_target="tpu_custom_call" | custom-call | flops 4294967296 | bytes 25165824 | tf_op jit(solution)/shard_map/inverse/pallas_call | solution.py:419
  349.2 81.2 %all-to-all-done.3 = bf16[16,16,64,128]{3,2,1,0:T(8,128)(2,1)} async-done(((bf16[16,16,64,128]{3,2,1,0:T(8,128)(2,1)}), bf16[16,16,64,128]{3,2,1,0:T(8,128)(2,1)}, u32[]{:S(2)}, u32[]{:S(2)}) %all-to-all-start.3) | async-done | bytes 4194336 | tf_op jit(solution)/shard_map/all_to_all | solution.py:466
  430.4 11.2 %inverse.3 = bf16[2,128,64,1024]{3,2,1,0:T(8,128)(2,1)} custom-call(bf16[4,4,16,64,128]{4,3,2,1,0:T(8,128)(2,1)} %bitcast.12.y_ref, bf16[256,1024]{1,0:T(8,128)(2,1)} %constant.48.clone.table_ref, bf16[2,128,64,1024]{3,2,1,0:T(8,128)(2,1)} %inverse.2.refs_0_), custom_call_target="tpu_custom_call", output_to_operand_aliasing={{}: (2, {})} | custom-call | flops 4294967296 | bytes 25165824 | tf_op jit(solution)/shard_map/inverse/pallas_call | solution.py:419
  (3 shorter events, 0.0 us)
Async XLA Ops:
  11.4 13.0 %collective-permute-start = (f32[2,64,1024]{2,1,0:T(8,128)}, f32[2,64,1024]{2,1,0:T(8,128)S(1)}, u32[]{:S(2)}, u32[]{:S(2)}) collective-permute-start(f32[2,64,1024]{2,1,0:T(8,128)} %stats.2.mine_ref), channel_id=1, source_target_pairs={{0,1},{1,0},{2,3},{3,2},{4,5},{5,4},{6,7},{7,6},{8,9},{9,8},{10,11... | collective-permute-start | bytes 1572872 | tf_op jit(solution)/shard_map/ppermute | solution.py:460
  24.4 0.8 copy-start.1
  38.4 99.9 %all-to-all-start = ((bf16[16,16,64,128]{3,2,1,0:T(8,128)(2,1)}), bf16[16,16,64,128]{3,2,1,0:T(8,128)(2,1)}, u32[]{:S(2)}, u32[]{:S(2)}) async-start(bf16[16,16,64,128]{3,2,1,0:T(8,128)(2,1)} %bitcast.33), calls=%async_computation | async-start | bytes 8388608 | tf_op jit(solution)/shard_map/all_to_all | solution.py:466
  57.2 13.5 %collective-permute-start.1 = (f32[2,64,1024]{2,1,0:T(8,128)}, f32[2,64,1024]{2,1,0:T(8,128)S(1)}, u32[]{:S(2)}, u32[]{:S(2)}) collective-permute-start(f32[2,64,1024]{2,1,0:T(8,128)} %stats.3.mine_ref), channel_id=1, source_target_pairs={{0,1},{1,0},{2,3},{3,2},{4,5},{5,4},{6,7},{7,6},{8,9},{9,8},{10,11... | collective-permute-start | bytes 1572872 | tf_op jit(solution)/shard_map/ppermute | solution.py:460
  70.7 0.8 copy-start
  138.3 97.4 %all-to-all-start.2 = ((bf16[16,16,64,128]{3,2,1,0:T(8,128)(2,1)}), bf16[16,16,64,128]{3,2,1,0:T(8,128)(2,1)}, u32[]{:S(2)}, u32[]{:S(2)}) async-start(bf16[16,16,64,128]{3,2,1,0:T(8,128)(2,1)} %bitcast.32), calls=%async_computation.2 | async-start | bytes 8388608 | tf_op jit(solution)/shard_map/all_to_all | solution.py:466
  143.2 3.4 copy-start.3
  143.2 3.4 copy-start.4
  143.2 3.4 copy-start.2
  235.6 97.4 %all-to-all-start.1 = ((bf16[16,16,64,128]{3,2,1,0:T(8,128)(2,1)}), bf16[16,16,64,128]{3,2,1,0:T(8,128)(2,1)}, u32[]{:S(2)}, u32[]{:S(2)}) async-start(bf16[16,16,64,128]{3,2,1,0:T(8,128)(2,1)} %spectral.2), calls=%async_computation.1 | async-start | bytes 8388608 | tf_op jit(solution)/shard_map/all_to_all | solution.py:466
  333.0 97.4 %all-to-all-start.3 = ((bf16[16,16,64,128]{3,2,1,0:T(8,128)(2,1)}), bf16[16,16,64,128]{3,2,1,0:T(8,128)(2,1)}, u32[]{:S(2)}, u32[]{:S(2)}) async-start(bf16[16,16,64,128]{3,2,1,0:T(8,128)(2,1)} %spectral.3), calls=%async_computation.3 | async-start | bytes 8388608 | tf_op jit(solution)/shard_map/all_to_all | solution.py:466

commit v2 on v1

--- a/solution.py
+++ b/solution.py
@@ -149,6 +149,7 @@
 
 LANES = 128
 HALF = LANES // 2
+TILE_ROWS = 256
 VMEM_BYTES = 56 * 1024 * 1024
 
 
@@ -198,27 +199,31 @@
     return jnp.where(is_real, turn(values, LANES - quarter), turn(values, quarter)), is_real
 
 
-def stats_kernel(field_ref, out_ref):
+def stats_kernel(field_ref, *refs):
+    out_ref = refs[-1]
     channels, rows, cols = field_ref.shape[1:]
-    zero = jnp.zeros((rows, cols), jnp.float32)
-
-    def add(c, total):
-        return total + field_ref[0, c].astype(jnp.float32)
-
-    mean = lax.fori_loop(0, channels, add, zero, unroll=8) * (1.0 / channels)
-
-    def add_square(c, total):
-        centered = field_ref[0, c].astype(jnp.float32) - mean
-        return total + centered * centered
-
-    out_ref[0] = mean
-    out_ref[1] = lax.fori_loop(0, channels, add_square, zero, unroll=8)
-
-
-def forward_kernel(field_ref, mine_ref, other_ref, gain_ref, table_ref, out_ref, average, inv_std, normed):
+    span = cols // 2
+    for start in range(0, cols, span):
+        lanes = slice(start, start + span)
+        pivot = field_ref[0, 0, :, lanes].astype(jnp.float32)
+        zero = jnp.zeros((rows, span), jnp.float32)
+
+        def add(c, totals):
+            moved = field_ref[0, c, :, lanes].astype(jnp.float32) - pivot
+            return totals[0] + moved, totals[1] + moved * moved
+
+        total, squares = lax.fori_loop(0, channels, add, (zero, zero), unroll=8)
+        offset = total * (1.0 / channels)
+        out_ref[0, :, lanes] = pivot + offset
+        out_ref[1, :, lanes] = jnp.maximum(squares - total * offset, 0.0)
+
+
+def forward_kernel(field_ref, mine_ref, other_ref, gain_ref, table_ref, *refs):
+    out_ref, average, inv_std, normed = refs[-4:]
     width, rows, cols = field_ref.shape[1:]
     half_width = width // 2
-    group = 4
+    group = min(half_width, TILE_ROWS // rows)
+    groups = half_width // group
     first = pl.program_id(0) * width
     gap = mine_ref[0] - other_ref[0]
     average[...] = (mine_ref[0] + other_ref[0]) * 0.5
@@ -226,8 +231,7 @@
     inv_std[...] = lax.rsqrt(variance + EPS)
     step = 16
 
-    @pl.loop(0, half_width // group)
-    def _(g):
+    def normalize(g):
         for side in range(2):
             for i in range(group):
                 c = side * half_width + g * group + i
@@ -237,14 +241,19 @@
                     x = field_ref[0, c, part, :].astype(jnp.float32)
                     value = (x - average[part, :]) * inv_std[part, :] * scale
                     at = (side * group + i) * rows + r
-                    normed[at : at + step, :] = value.astype(jnp.bfloat16)
-        y = jnp.dot(normed[...], table_ref[...], preferred_element_type=jnp.float32)
+                    normed[g, at : at + step, :] = value.astype(jnp.bfloat16)
+
+    normalize(0)
+    for g in range(groups):
+        if g + 1 < groups:
+            normalize(g + 1)
+        y = jnp.dot(normed[g], table_ref[...], preferred_element_type=jnp.float32)
         low, high = y[: group * rows], y[group * rows :]
         for p in range(2):
             lanes = slice(p * LANES, (p + 1) * LANES)
             even, odd = exchange_halves(low[:, lanes], high[:, lanes])
             for q, packed in ((2 * p, even), (2 * p + 1, odd)):
-                out_ref[0, q, pl.ds(g * group, group)] = packed.astype(jnp.bfloat16).reshape(
+                out_ref[0, q, g * group : (g + 1) * group] = packed.astype(jnp.bfloat16).reshape(
                     group, rows, LANES
                 )
 
@@ -314,14 +323,12 @@
 def inverse_kernel(y_ref, table_ref, *refs):
     out_ref = refs[-1]
     pairs, rows = y_ref.shape[2:4]
-    group = 4
-
-    @pl.loop(0, pairs // group)
-    def _(g):
+    group = min(pairs, TILE_ROWS // rows)
+    for at in range(0, pairs, group):
         sides = ([], [])
         for p in range(2):
             parts = [
-                y_ref[0, 2 * p + i, pl.ds(g * group, group)]
+                y_ref[0, 2 * p + i, at : at + group]
                 .reshape(group * rows, LANES)
                 .astype(jnp.float32)
                 for i in range(2)
@@ -332,9 +339,9 @@
             mixed = jnp.dot(
                 jnp.concatenate(side, axis=1), table_ref[...], preferred_element_type=jnp.float32
             )
-            out_ref[0, pl.ds(s * pairs + g * group, group)] = mixed.astype(jnp.bfloat16).reshape(
-                group, rows, mixed.shape[1]
-            )
+            out_ref[0, s * pairs + at : s * pairs + at + group] = mixed.astype(
+                jnp.bfloat16
+            ).reshape(group, rows, mixed.shape[1])
 
 
 def params(count):
@@ -347,46 +354,62 @@
     return pl.CostEstimate(flops=flops, bytes_accessed=moved, transcendentals=0)
 
 
-def local_stats(field, index):
+def local_stats(field, index, part, parts, after):
     _, channels, rows, cols = field.shape
     step = 16
+    rows //= parts
+    steps = rows // step
     return pl.pallas_call(
         stats_kernel,
-        grid=(rows // step,),
-        in_specs=[pl.BlockSpec((1, channels, step, cols), lambda i: (index, 0, i, 0))],
+        grid=(steps,),
+        in_specs=[
+            pl.BlockSpec((1, channels, step, cols), lambda i: (index, 0, part * steps + i, 0))
+        ]
+        + [pl.BlockSpec(memory_space=pl.ANY)] * len(after),
         out_specs=pl.BlockSpec((2, step, cols), lambda i: (0, i, 0)),
         out_shape=jax.ShapeDtypeStruct((2, rows, cols), jnp.float32),
         compiler_params=params(1),
         cost_estimate=cost(5 * channels * rows * cols, 2 * channels * rows * cols),
         name="stats",
-    )(field)
-
-
-def forward_part(field, index, mine, other, gain, table, width):
-    _, channels, rows, cols = field.shape
+    )(field, *after)
+
+
+def forward_part(field, index, part, parts, stats, gain, table, width, so_far):
+    _, channels, all_rows, cols = field.shape
+    rows = all_rows // parts
     blocks = channels // width
+    half_width = width // 2
+    group = min(half_width, TILE_ROWS // rows)
     whole = lambda *shape: pl.BlockSpec(shape, lambda i: (0,) * len(shape))
+    operands = [field, *stats, gain, table]
+    specs = [
+        pl.BlockSpec((1, width, rows, cols), lambda i: (index, i, part, 0)),
+        whole(2, rows, cols),
+        whole(2, rows, cols),
+        pl.BlockSpec(memory_space=pltpu.SMEM),
+        whole(*table.shape),
+    ]
+    aliases = {}
+    if so_far is not None:
+        aliases = {len(operands): 0}
+        operands.append(so_far)
+        specs.append(pl.BlockSpec(memory_space=pl.ANY))
     return pl.pallas_call(
         forward_kernel,
         grid=(blocks,),
-        in_specs=[
-            pl.BlockSpec((1, width, rows, cols), lambda i: (index, i, 0, 0)),
-            whole(2, rows, cols),
-            whole(2, rows, cols),
-            pl.BlockSpec(memory_space=pltpu.SMEM),
-            whole(*table.shape),
-        ],
-        out_specs=pl.BlockSpec((1, 4, width // 2, rows, LANES), lambda i: (i, 0, 0, 0, 0)),
-        out_shape=jax.ShapeDtypeStruct((blocks, 4, width // 2, rows, LANES), jnp.bfloat16),
+        in_specs=specs,
+        out_specs=pl.BlockSpec((1, 4, half_width, rows, LANES), lambda i: (i, 0, 0, part, 0)),
+        out_shape=jax.ShapeDtypeStruct((blocks, 4, half_width, all_rows, LANES), jnp.bfloat16),
+        input_output_aliases=aliases,
         scratch_shapes=[
             pltpu.VMEM((rows, cols), jnp.float32),
             pltpu.VMEM((rows, cols), jnp.float32),
-            pltpu.VMEM((8 * rows, cols), jnp.bfloat16),
+            pltpu.VMEM((half_width // group, 2 * group * rows, cols), jnp.bfloat16),
         ],
         compiler_params=params(1),
         cost_estimate=cost(4 * MODES_X * channels * rows * cols, 3 * channels * rows * cols),
         name="forward",
-    )(field, mine, other, gain, table)
+    )(*operands)
 
 
 def spectral_part(columns, fwd, inv, weights_one, bias_one, weights_two, bias_two, repeat):
@@ -408,9 +431,10 @@
     blocks, parts, pairs, rows, _ = received.shape
     slices, channels, _, cols = shape
     width = 2 * pairs
+    step = rows // 2
     operands, specs, aliases = [received, table], [
-        pl.BlockSpec((1, parts, pairs, rows, LANES), lambda i: (i, 0, 0, 0, 0)),
-        pl.BlockSpec(table.shape, lambda i: (0, 0)),
+        pl.BlockSpec((1, parts, pairs, step, LANES), lambda i, j: (i, 0, 0, j, 0)),
+        pl.BlockSpec(table.shape, lambda i, j: (0, 0)),
     ], {}
     if so_far is not None:
         operands.append(so_far)
@@ -418,12 +442,12 @@
         aliases = {2: 0}
     return pl.pallas_call(
         inverse_kernel,
-        grid=(blocks,),
+        grid=(blocks, rows // step),
         in_specs=specs,
-        out_specs=pl.BlockSpec((1, width, rows, cols), lambda i: (index, i, 0, 0)),
+        out_specs=pl.BlockSpec((1, width, step, cols), lambda i, j: (index, i, j, 0)),
         out_shape=jax.ShapeDtypeStruct(shape, jnp.bfloat16),
         input_output_aliases=aliases,
-        compiler_params=params(1),
+        compiler_params=params(2),
         cost_estimate=cost(4 * MODES_X * channels * rows * cols, 3 * channels * rows * cols),
         name="inverse",
     )(*operands)
@@ -454,13 +478,21 @@
 
     layers = (spread(w_first), widen(b_first), spread(w_second), widen(b_second))
     swap = [(0, 1), (1, 0)]
-    packed, others = [], []
+    parts = [2] + [1] * (slices - 1)
+    packed, after = [], []
     for b in range(slices):
-        mine = local_stats(field, b)
-        others.append((mine, lax.ppermute(mine, "blk", swap)))
-    for b, (mine, other) in enumerate(others):
-        part = forward_part(field, b, mine, other, gain, fwd_cols, width)
-        packed.append(part.reshape((-1,) + part.shape[2:]))
+        stats = []
+        for part in range(parts[b]):
+            mine = local_stats(field, b, part, parts[b], after)
+            stats.append((mine, lax.ppermute(mine, "blk", swap)))
+            after = [mine]
+        result = None
+        for part, pair in enumerate(stats):
+            result = forward_part(
+                field, b, part, parts[b], pair, gain, fwd_cols, width, result
+            )
+        after = [result]
+        packed.append(result.reshape((-1,) + result.shape[2:]))
 
     def send(values):
         return lax.all_to_all(values, "row", split_axis=0, concat_axis=0, tiled=True)
@@ -486,7 +518,7 @@
 
 def packs(mesh, channels, width):
     groups, owners = mesh.shape["blk"], mesh.shape["row"]
-    return groups == 2 and owners == 4 * (channels // groups // width) and HEIGHT % (16 * owners) == 0
+    return groups == 2 and owners == 4 * (channels // groups // width) and HEIGHT % (32 * owners) == 0
 
 
 def solution(mesh):

time: 443 us -> 435 us (0.982)
  waiting for transfers between devices: 267 us -> 257 us
    ppermute x2 -> x3, waiting for transfers between devices: 24 us -> 12.3 us  [local_packed(): stats.append((mine, lax.ppermute(mine, 'blk', swap)))]
    pallas_call x6 -> x8, Pallas kernels: 71.6 us -> 72.5 us  [the longest x3 27.6 us: forward_part(): pl.pallas_call(forward_kernel, grid=(blocks,), in_specs=specs, out_specs=...]
  transfers between devices with their start and end apart: 6 -> 7, of which waited for: 6 -> 5; matrix products, arithmetic and copies ran while one was open for 1% -> 1% of each run, Pallas kernels for 24% -> 27%
where the time goes in v2:
time: 435 us; the launch traced here: 434 us
  waiting for transfers between devices  257 us (59%)
  Pallas kernels  144 us (33%)
  starting transfers between devices  24.7 us (6%)
  local copies, waits for them, and re-layouts  6.84 us (2%)
    all_to_all x4, waiting for transfers between devices, send(): lax.all_to_all(values, 'row', split_axis=0, concat_axis=0, tiled=True)  245 us
    pallas_call x2, Pallas kernels, spectral_part(): pl.pallas_call(lambda *refs: spectral_kernel(*refs, repeat), in_specs=[vm...  71.4 us
    pallas_call x3, Pallas kernels, forward_part(): pl.pallas_call(forward_kernel, grid=(blocks,), in_specs=specs, out_specs=...  27.6 us
    pallas_call x2, Pallas kernels, inverse_part(): pl.pallas_call(inverse_kernel, grid=(blocks, rows // step), in_specs=spec...  22.8 us
    pallas_call x3, Pallas kernels, local_stats(): pl.pallas_call(stats_kernel, grid=(steps,), in_specs=[pl.BlockSpec((1, ch...  22.1 us
    all_to_all x4, starting transfers between devices, send(): lax.all_to_all(values, 'row', split_axis=0, concat_axis=0, tiled=True)  22.1 us
    ppermute x3, waiting for transfers between devices, local_packed(): stats.append((mine, lax.ppermute(mine, 'blk', swap)))  12.3 us
  transfers between devices with their start and end apart: 7, of which 5 were waited for; matrix products, arithmetic and copies ran while one was open for 1% of the time, Pallas kernels for 27%

profile of v2, /device:TPU:13, one launch (start us, length us, event | category | flops | bytes accessed | tf_op | source)
XLA Modules:
  0.0 433.7 jit_solution(17187257874579227629)
XLA Ops:
  0.0 6.0 %stats.3.refs_0_.mine_ref = f32[2,32,1024]{2,1,0:T(8,128)} custom-call(bf16[2,128,64,1024]{3,2,1,0:T(8,128)(2,1)} %field_ref.11), custom_call_target="tpu_custom_call" | custom-call | flops 20971520 | bytes 8388608 | tf_op jit(solution)/shard_map/stats/pallas_call | solution.py:362
  6.0 1.2 collective-permute-start.1
  7.3 6.0 %stats.4.mine_ref = f32[2,32,1024]{2,1,0:T(8,128)} custom-call(bf16[2,128,64,1024]{3,2,1,0:T(8,128)(2,1)} %field_ref.11, f32[2,32,1024]{2,1,0:T(8,128)} %stats.3.refs_0_.mine_ref), custom_call_target="tpu_custom_call" | custom-call | flops 20971520 | bytes 8388608 | tf_op jit(solution)/shard_map/stats/pallas_call | solution.py:362
  13.3 0.3 collective-permute-start
  13.5 0.0 collective-permute-done.1.other_ref
  13.5 0.0 copy-start.2
  13.5 0.7 copy-done.2
  14.2 7.7 %forward.3.refs_0_ = bf16[4,4,16,64,128]{4,3,2,1,0:T(8,128)(2,1)} custom-call(bf16[2,128,64,1024]{3,2,1,0:T(8,128)(2,1)} %field_ref.11, f32[2,32,1024]{2,1,0:T(8,128)} %stats.3.refs_0_.mine_ref, f32[2,32,1024]{2,1,0:T(8,128)} %copy-done.2, f32[128]{0:T(128)} %gain_ref.5, bf16[1024,256]{1,0:T(8,128)(2,1)} %constant.47.clone.table_ref), custom_call_target="tpu_custom_call" | custom-call | flops 2147483648 | bytes 12582912 | tf_op jit(solution)/shard_map/forward/pallas_call | solution.py:397
  21.9 0.0 collective-permute-done.other_ref
  21.9 0.0 copy-start.1
  22.0 0.7 copy-done.1
  22.7 7.7 %forward.4.refs_0_ = bf16[4,4,16,64,128]{4,3,2,1,0:T(8,128)(2,1)} custom-call(bf16[2,128,64,1024]{3,2,1,0:T(8,128)(2,1)} %field_ref.11, f32[2,32,1024]{2,1,0:T(8,128)} %stats.4.mine_ref, f32[2,32,1024]{2,1,0:T(8,128)} %copy-done.1, f32[128]{0:T(128)} %gain_ref.5, bf16[1024,256]{1,0:T(8,128)(2,1)} %constant.47.clone.table_ref, ...), custom_call_target="tpu_custom_call", output_to_operand_aliasing={{}: (5, {})} | custom-call | flops 2147483648 | bytes 12582912 | tf_op jit(solution)/shard_map/forward/pallas_call | solution.py:397
  30.4 7.3 %all-to-all-start = ((bf16[16,16,64,128]{3,2,1,0:T(8,128)(2,1)}), bf16[16,16,64,128]{3,2,1,0:T(8,128)(2,1)}, u32[]{:S(2)}, u32[]{:S(2)}) async-start(bf16[16,16,64,128]{3,2,1,0:T(8,128)(2,1)} %bitcast.32), calls=%async_computation | async-start | bytes 8388608 | tf_op jit(solution)/shard_map/all_to_all | solution.py:498
  37.7 10.1 %stats.5.mine_ref = f32[2,64,1024]{2,1,0:T(8,128)} custom-call(bf16[2,128,64,1024]{3,2,1,0:T(8,128)(2,1)} %field_ref.11, bf16[4,4,16,64,128]{4,3,2,1,0:T(8,128)(2,1)} %forward.4.refs_0_), custom_call_target="tpu_custom_call" | custom-call | flops 41943040 | bytes 16777216 | tf_op jit(solution)/shard_map/stats/pallas_call | solution.py:362
  47.8 1.2 collective-permute-start.2
  49.0 12.3 %collective-permute-done.2.other_ref = f32[2,64,1024]{2,1,0:T(8,128)S(1)} collective-permute-done((f32[2,64,1024]{2,1,0:T(8,128)}, f32[2,64,1024]{2,1,0:T(8,128)S(1)}, u32[]{:S(2)}, u32[]{:S(2)}) %collective-permute-start.2) | collective-permute-done | bytes 524320 | tf_op jit(solution)/shard_map/ppermute | solution.py:487
  61.2 0.8 copy-done
  62.0 12.2 %forward.5 = bf16[4,4,16,64,128]{4,3,2,1,0:T(8,128)(2,1)} custom-call(bf16[2,128,64,1024]{3,2,1,0:T(8,128)(2,1)} %field_ref.11, f32[2,64,1024]{2,1,0:T(8,128)} %stats.5.mine_ref, f32[2,64,1024]{2,1,0:T(8,128)} %copy-done, f32[128]{0:T(128)} %gain_ref.5, bf16[1024,256]{1,0:T(8,128)(2,1)} %constant.47.clone.table_ref), custom_call_target="tpu_custom_call" | custom-call | flops 4294967296 | bytes 25165824 | tf_op jit(solution)/shard_map/forward/pallas_call | solution.py:397
  74.2 56.0 %all-to-all-done.refs_0_ = bf16[16,16,64,128]{3,2,1,0:T(8,128)(2,1)} async-done(((bf16[16,16,64,128]{3,2,1,0:T(8,128)(2,1)}), bf16[16,16,64,128]{3,2,1,0:T(8,128)(2,1)}, u32[]{:S(2)}, u32[]{:S(2)}) %all-to-all-start) | async-done | bytes 4194336 | tf_op jit(solution)/shard_map/all_to_all | solution.py:498
  130.2 4.9 %all-to-all-start.2 = ((bf16[16,16,64,128]{3,2,1,0:T(8,128)(2,1)}), bf16[16,16,64,128]{3,2,1,0:T(8,128)(2,1)}, u32[]{:S(2)}, u32[]{:S(2)}) async-start(bf16[16,16,64,128]{3,2,1,0:T(8,128)(2,1)} %bitcast.33), calls=%async_computation.2 | async-start | bytes 8388608 | tf_op jit(solution)/shard_map/all_to_all | solution.py:498
  135.1 0.0 copy-start.5
  135.1 0.0 copy-start.3
  135.1 0.7 dynamic-slice_bitcast_fusion
  135.9 0.1 copy.18
  136.0 0.1 copy.16
  136.1 0.1 mul.47
  136.2 0.4 mul.48
  136.6 0.2 mul.51
  136.8 0.7 mul.52
  137.5 0.2 mul.55
  137.7 0.7 mul.56
  138.4 0.0 copy-done.4
  138.4 0.0 copy-done.5
  138.5 0.1 constant_dynamic-slice_fusion
  138.5 0.0 copy-done.3
  138.6 0.1 broadcast_select_fusion
  138.6 0.9 broadcast_multiply_fusion
  139.5 0.7 tile.20
  140.2 0.7 tile.8
  140.9 35.7 %spectral.2 = bf16[16,16,64,128]{3,2,1,0:T(8,128)(2,1)} custom-call(bf16[16,16,64,128]{3,2,1,0:T(8,128)(2,1)} %all-to-all-done.refs_0_, bf16[1024,1024]{1,0:T(8,128)(2,1)} %constant.49.clone.refs_1_, bf16[1024,1024]{1,0:T(8,128)(2,1)} %constant.50.clone.refs_2_, bf16[2,256,256]{2,1,0:T(8,128)(2,1)} %get-tuple-element.14.refs_3_, f32[256,128]{1,0:T(8,128)} %bitcast.36, ...), custom_call_target="tpu_custom_call" | custom-call | flops 12884901888 | bytes 8388608 | tf_op jit(solution)/shard_map/spectral/pallas_call | solution.py:418
  176.6 51.0 %all-to-all-done.2.refs_0_ = bf16[16,16,64,128]{3,2,1,0:T(8,128)(2,1)} async-done(((bf16[16,16,64,128]{3,2,1,0:T(8,128)(2,1)}), bf16[16,16,64,128]{3,2,1,0:T(8,128)(2,1)}, u32[]{:S(2)}, u32[]{:S(2)}) %all-to-all-start.2) | async-done | bytes 4194336 | tf_op jit(solution)/shard_map/all_to_all | solution.py:498
  227.6 4.9 %all-to-all-start.1 = ((bf16[16,16,64,128]{3,2,1,0:T(8,128)(2,1)}), bf16[16,16,64,128]{3,2,1,0:T(8,128)(2,1)}, u32[]{:S(2)}, u32[]{:S(2)}) async-start(bf16[16,16,64,128]{3,2,1,0:T(8,128)(2,1)} %spectral.2), calls=%async_computation.1 | async-start | bytes 8388608 | tf_op jit(solution)/shard_map/all_to_all | solution.py:498
  232.5 35.7 %spectral.3 = bf16[16,16,64,128]{3,2,1,0:T(8,128)(2,1)} custom-call(bf16[16,16,64,128]{3,2,1,0:T(8,128)(2,1)} %all-to-all-done.2.refs_0_, bf16[1024,1024]{1,0:T(8,128)(2,1)} %constant.49.clone.refs_1_, bf16[1024,1024]{1,0:T(8,128)(2,1)} %constant.50.clone.refs_2_, bf16[2,256,256]{2,1,0:T(8,128)(2,1)} %get-tuple-element.14.refs_3_, f32[256,128]{1,0:T(8,128)} %bitcast.37, ...), custom_call_target="tpu_custom_call" | custom-call | flops 12884901888 | bytes 8388608 | tf_op jit(solution)/shard_map/spectral/pallas_call | solution.py:418
  268.1 56.8 %all-to-all-done.1 = bf16[16,16,64,128]{3,2,1,0:T(8,128)(2,1)} async-done(((bf16[16,16,64,128]{3,2,1,0:T(8,128)(2,1)}), bf16[16,16,64,128]{3,2,1,0:T(8,128)(2,1)}, u32[]{:S(2)}, u32[]{:S(2)}) %all-to-all-start.1) | async-done | bytes 4194336 | tf_op jit(solution)/shard_map/all_to_all | solution.py:498
  324.9 4.9 %all-to-all-start.3 = ((bf16[16,16,64,128]{3,2,1,0:T(8,128)(2,1)}), bf16[16,16,64,128]{3,2,1,0:T(8,128)(2,1)}, u32[]{:S(2)}, u32[]{:S(2)}) async-start(bf16[16,16,64,128]{3,2,1,0:T(8,128)(2,1)} %spectral.3), calls=%async_computation.3 | async-start | bytes 8388608 | tf_op jit(solution)/shard_map/all_to_all | solution.py:498
  329.8 11.4 %inverse.2.refs_0_ = bf16[2,128,64,1024]{3,2,1,0:T(8,128)(2,1)} custom-call(bf16[4,4,16,64,128]{4,3,2,1,0:T(8,128)(2,1)} %bitcast.13.y_ref, bf16[256,1024]{1,0:T(8,128)(2,1)} %constant.48.clone.table_ref), custom_call_target="tpu_custom_call" | custom-call | flops 4294967296 | bytes 25165824 | tf_op jit(solution)/shard_map/inverse/pallas_call | solution.py:443
  341.2 81.1 %all-to-all-done.3 = bf16[16,16,64,128]{3,2,1,0:T(8,128)(2,1)} async-done(((bf16[16,16,64,128]{3,2,1,0:T(8,128)(2,1)}), bf16[16,16,64,128]{3,2,1,0:T(8,128)(2,1)}, u32[]{:S(2)}, u32[]{:S(2)}) %all-to-all-start.3) | async-done | bytes 4194336 | tf_op jit(solution)/shard_map/all_to_all | solution.py:498
  422.3 11.4 %inverse.3 = bf16[2,128,64,1024]{3,2,1,0:T(8,128)(2,1)} custom-call(bf16[4,4,16,64,128]{4,3,2,1,0:T(8,128)(2,1)} %bitcast.12.y_ref, bf16[256,1024]{1,0:T(8,128)(2,1)} %constant.48.clone.table_ref, bf16[2,128,64,1024]{3,2,1,0:T(8,128)(2,1)} %inverse.2.refs_0_), custom_call_target="tpu_custom_call", output_to_operand_aliasing={{}: (2, {})} | custom-call | flops 4294967296 | bytes 25165824 | tf_op jit(solution)/shard_map/inverse/pallas_call | solution.py:443
  (5 shorter events, 0.0 us)
Async XLA Ops:
  6.0 7.5 %collective-permute-start.1 = (f32[2,32,1024]{2,1,0:T(8,128)}, f32[2,32,1024]{2,1,0:T(8,128)S(1)}, u32[]{:S(2)}, u32[]{:S(2)}) collective-permute-start(f32[2,32,1024]{2,1,0:T(8,128)} %stats.3.refs_0_.mine_ref), channel_id=1, source_target_pairs={{0,1},{1,0},{2,3},{3,2},{4,5},{5,4},{6,7},{7,6},{8,9},{9,8},{10,11... | collective-permute-start | bytes 786440 | tf_op jit(solution)/shard_map/ppermute | solution.py:487
  13.3 8.7 %collective-permute-start = (f32[2,32,1024]{2,1,0:T(8,128)}, f32[2,32,1024]{2,1,0:T(8,128)S(1)}, u32[]{:S(2)}, u32[]{:S(2)}) collective-permute-start(f32[2,32,1024]{2,1,0:T(8,128)} %stats.4.mine_ref), channel_id=1, source_target_pairs={{0,1},{1,0},{2,3},{3,2},{4,5},{5,4},{6,7},{7,6},{8,9},{9,8},{10,11... | collective-permute-start | bytes 786440 | tf_op jit(solution)/shard_map/ppermute | solution.py:487
  13.5 0.7 copy-start.2
  21.9 0.7 copy-start.1
  30.4 99.8 %all-to-all-start = ((bf16[16,16,64,128]{3,2,1,0:T(8,128)(2,1)}), bf16[16,16,64,128]{3,2,1,0:T(8,128)(2,1)}, u32[]{:S(2)}, u32[]{:S(2)}) async-start(bf16[16,16,64,128]{3,2,1,0:T(8,128)(2,1)} %bitcast.32), calls=%async_computation | async-start | bytes 8388608 | tf_op jit(solution)/shard_map/all_to_all | solution.py:498
  47.8 13.5 %collective-permute-start.2 = (f32[2,64,1024]{2,1,0:T(8,128)}, f32[2,64,1024]{2,1,0:T(8,128)S(1)}, u32[]{:S(2)}, u32[]{:S(2)}) collective-permute-start(f32[2,64,1024]{2,1,0:T(8,128)} %stats.5.mine_ref), channel_id=1, source_target_pairs={{0,1},{1,0},{2,3},{3,2},{4,5},{5,4},{6,7},{7,6},{8,9},{9,8},{10,11... | collective-permute-start | bytes 1572872 | tf_op jit(solution)/shard_map/ppermute | solution.py:487
  61.2 0.8 copy-start
  130.2 97.4 %all-to-all-start.2 = ((bf16[16,16,64,128]{3,2,1,0:T(8,128)(2,1)}), bf16[16,16,64,128]{3,2,1,0:T(8,128)(2,1)}, u32[]{:S(2)}, u32[]{:S(2)}) async-start(bf16[16,16,64,128]{3,2,1,0:T(8,128)(2,1)} %bitcast.33), calls=%async_computation.2 | async-start | bytes 8388608 | tf_op jit(solution)/shard_map/all_to_all | solution.py:498
  135.1 3.4 copy-start.4
  135.1 3.4 copy-start.5
  135.1 3.4 copy-start.3
  227.6 97.4 %all-to-all-start.1 = ((bf16[16,16,64,128]{3,2,1,0:T(8,128)(2,1)}), bf16[16,16,64,128]{3,2,1,0:T(8,128)(2,1)}, u32[]{:S(2)}, u32[]{:S(2)}) async-start(bf16[16,16,64,128]{3,2,1,0:T(8,128)(2,1)} %spectral.2), calls=%async_computation.1 | async-start | bytes 8388608 | tf_op jit(solution)/shard_map/all_to_all | solution.py:498
  324.9 97.4 %all-to-all-start.3 = ((bf16[16,16,64,128]{3,2,1,0:T(8,128)(2,1)}), bf16[16,16,64,128]{3,2,1,0:T(8,128)(2,1)}, u32[]{:S(2)}, u32[]{:S(2)}) async-start(bf16[16,16,64,128]{3,2,1,0:T(8,128)(2,1)} %spectral.3), calls=%async_computation.3 | async-start | bytes 8388608 | tf_op jit(solution)/shard_map/all_to_all | solution.py:498

commit v3 on v2

--- a/solution.py
+++ b/solution.py
@@ -502,11 +502,8 @@
     for b in range(slices):
         following = None
         if b + 1 < slices:
-            columns, ready = lax.optimization_barrier((columns, packed[b + 1]))
-            following = send(ready)
+            following = send(packed[b + 1])
         filtered = spectral_part(columns, fwd_rows, inv_rows, *layers, repeat)
-        if received:
-            received[-1], filtered = lax.optimization_barrier((received[-1], filtered))
         received.append(send(filtered))
         columns = following
     mixed = None

time: 435 us -> 435 us (level)
  no operation moved by 1% of the time
where the time goes in v3:
time: 435 us; the launch traced here: 434 us
  waiting for transfers between devices  257 us (59%)
  Pallas kernels  144 us (33%)
  starting transfers between devices  24.7 us (6%)
  local copies, waits for them, and re-layouts  6.84 us (2%)
    all_to_all x4, waiting for transfers between devices, send(): lax.all_to_all(values, 'row', split_axis=0, concat_axis=0, tiled=True)  245 us
    pallas_call x2, Pallas kernels, spectral_part(): pl.pallas_call(lambda *refs: spectral_kernel(*refs, repeat), in_specs=[vm...  71.4 us
    pallas_call x3, Pallas kernels, forward_part(): pl.pallas_call(forward_kernel, grid=(blocks,), in_specs=specs, out_specs=...  27.6 us
    pallas_call x2, Pallas kernels, inverse_part(): pl.pallas_call(inverse_kernel, grid=(blocks, rows // step), in_specs=spec...  22.8 us
    pallas_call x3, Pallas kernels, local_stats(): pl.pallas_call(stats_kernel, grid=(steps,), in_specs=[pl.BlockSpec((1, ch...  22.1 us
    all_to_all x4, starting transfers between devices, send(): lax.all_to_all(values, 'row', split_axis=0, concat_axis=0, tiled=True)  22.1 us
    ppermute x3, waiting for transfers between devices, local_packed(): stats.append((mine, lax.ppermute(mine, 'blk', swap)))  12.3 us
  transfers between devices with their start and end apart: 7, of which 5 were waited for; matrix products, arithmetic and copies ran while one was open for 1% of the time, Pallas kernels for 27%

profile of v3, /device:TPU:13, one launch (start us, length us, event | category | flops | bytes accessed | tf_op | source)
XLA Modules:
  0.0 433.7 jit_solution(17187257874579227629)
XLA Ops:
  0.0 6.0 %stats.3.refs_0_.mine_ref = f32[2,32,1024]{2,1,0:T(8,128)} custom-call(bf16[2,128,64,1024]{3,2,1,0:T(8,128)(2,1)} %field_ref.11), custom_call_target="tpu_custom_call" | custom-call | flops 20971520 | bytes 8388608 | tf_op jit(solution)/shard_map/stats/pallas_call | solution.py:362
  6.0 1.2 collective-permute-start.1
  7.3 6.0 %stats.4.mine_ref = f32[2,32,1024]{2,1,0:T(8,128)} custom-call(bf16[2,128,64,1024]{3,2,1,0:T(8,128)(2,1)} %field_ref.11, f32[2,32,1024]{2,1,0:T(8,128)} %stats.3.refs_0_.mine_ref), custom_call_target="tpu_custom_call" | custom-call | flops 20971520 | bytes 8388608 | tf_op jit(solution)/shard_map/stats/pallas_call | solution.py:362
  13.3 0.3 collective-permute-start
  13.5 0.0 collective-permute-done.1.other_ref
  13.5 0.0 copy-start.2
  13.5 0.7 copy-done.2
  14.2 7.7 %forward.3.refs_0_ = bf16[4,4,16,64,128]{4,3,2,1,0:T(8,128)(2,1)} custom-call(bf16[2,128,64,1024]{3,2,1,0:T(8,128)(2,1)} %field_ref.11, f32[2,32,1024]{2,1,0:T(8,128)} %stats.3.refs_0_.mine_ref, f32[2,32,1024]{2,1,0:T(8,128)} %copy-done.2, f32[128]{0:T(128)} %gain_ref.5, bf16[1024,256]{1,0:T(8,128)(2,1)} %constant.47.clone.table_ref), custom_call_target="tpu_custom_call" | custom-call | flops 2147483648 | bytes 12582912 | tf_op jit(solution)/shard_map/forward/pallas_call | solution.py:397
  21.9 0.0 collective-permute-done.other_ref
  21.9 0.0 copy-start.1
  22.0 0.7 copy-done.1
  22.7 7.7 %forward.4.refs_0_ = bf16[4,4,16,64,128]{4,3,2,1,0:T(8,128)(2,1)} custom-call(bf16[2,128,64,1024]{3,2,1,0:T(8,128)(2,1)} %field_ref.11, f32[2,32,1024]{2,1,0:T(8,128)} %stats.4.mine_ref, f32[2,32,1024]{2,1,0:T(8,128)} %copy-done.1, f32[128]{0:T(128)} %gain_ref.5, bf16[1024,256]{1,0:T(8,128)(2,1)} %constant.47.clone.table_ref, ...), custom_call_target="tpu_custom_call", output_to_operand_aliasing={{}: (5, {})} | custom-call | flops 2147483648 | bytes 12582912 | tf_op jit(solution)/shard_map/forward/pallas_call | solution.py:397
  30.4 7.3 %all-to-all-start.2 = ((bf16[16,16,64,128]{3,2,1,0:T(8,128)(2,1)}), bf16[16,16,64,128]{3,2,1,0:T(8,128)(2,1)}, u32[]{:S(2)}, u32[]{:S(2)}) async-start(bf16[16,16,64,128]{3,2,1,0:T(8,128)(2,1)} %bitcast.32), calls=%async_computation.2 | async-start | bytes 8388608 | tf_op jit(solution)/shard_map/all_to_all | solution.py:498
  37.7 10.1 %stats.5.mine_ref = f32[2,64,1024]{2,1,0:T(8,128)} custom-call(bf16[2,128,64,1024]{3,2,1,0:T(8,128)(2,1)} %field_ref.11, bf16[4,4,16,64,128]{4,3,2,1,0:T(8,128)(2,1)} %forward.4.refs_0_), custom_call_target="tpu_custom_call" | custom-call | flops 41943040 | bytes 16777216 | tf_op jit(solution)/shard_map/stats/pallas_call | solution.py:362
  47.8 1.2 collective-permute-start.2
  49.0 12.3 %collective-permute-done.2.other_ref = f32[2,64,1024]{2,1,0:T(8,128)S(1)} collective-permute-done((f32[2,64,1024]{2,1,0:T(8,128)}, f32[2,64,1024]{2,1,0:T(8,128)S(1)}, u32[]{:S(2)}, u32[]{:S(2)}) %collective-permute-start.2) | collective-permute-done | bytes 524320 | tf_op jit(solution)/shard_map/ppermute | solution.py:487
  61.2 0.8 copy-done
  62.0 12.2 %forward.5 = bf16[4,4,16,64,128]{4,3,2,1,0:T(8,128)(2,1)} custom-call(bf16[2,128,64,1024]{3,2,1,0:T(8,128)(2,1)} %field_ref.11, f32[2,64,1024]{2,1,0:T(8,128)} %stats.5.mine_ref, f32[2,64,1024]{2,1,0:T(8,128)} %copy-done, f32[128]{0:T(128)} %gain_ref.5, bf16[1024,256]{1,0:T(8,128)(2,1)} %constant.47.clone.table_ref), custom_call_target="tpu_custom_call" | custom-call | flops 4294967296 | bytes 25165824 | tf_op jit(solution)/shard_map/forward/pallas_call | solution.py:397
  74.2 56.0 %all-to-all-done.2.refs_0_ = bf16[16,16,64,128]{3,2,1,0:T(8,128)(2,1)} async-done(((bf16[16,16,64,128]{3,2,1,0:T(8,128)(2,1)}), bf16[16,16,64,128]{3,2,1,0:T(8,128)(2,1)}, u32[]{:S(2)}, u32[]{:S(2)}) %all-to-all-start.2) | async-done | bytes 4194336 | tf_op jit(solution)/shard_map/all_to_all | solution.py:498
  130.2 4.9 %all-to-all-start = ((bf16[16,16,64,128]{3,2,1,0:T(8,128)(2,1)}), bf16[16,16,64,128]{3,2,1,0:T(8,128)(2,1)}, u32[]{:S(2)}, u32[]{:S(2)}) async-start(bf16[16,16,64,128]{3,2,1,0:T(8,128)(2,1)} %bitcast.33), calls=%async_computation | async-start | bytes 8388608 | tf_op jit(solution)/shard_map/all_to_all | solution.py:498
  135.1 0.0 copy-start.5
  135.1 0.0 copy-start.3
  135.1 0.7 dynamic-slice_bitcast_fusion
  135.9 0.1 copy.18
  136.0 0.1 copy.16
  136.1 0.1 mul.47
  136.2 0.4 mul.48
  136.6 0.2 mul.51
  136.8 0.7 mul.52
  137.5 0.2 mul.55
  137.7 0.7 mul.56
  138.4 0.0 copy-done.4
  138.4 0.0 copy-done.5
  138.5 0.1 constant_dynamic-slice_fusion
  138.5 0.0 copy-done.3
  138.6 0.1 broadcast_select_fusion
  138.6 0.9 broadcast_multiply_fusion
  139.5 0.7 tile.20
  140.2 0.7 tile.8
  140.9 35.7 %spectral.3 = bf16[16,16,64,128]{3,2,1,0:T(8,128)(2,1)} custom-call(bf16[16,16,64,128]{3,2,1,0:T(8,128)(2,1)} %all-to-all-done.2.refs_0_, bf16[1024,1024]{1,0:T(8,128)(2,1)} %constant.49.clone.refs_1_, bf16[1024,1024]{1,0:T(8,128)(2,1)} %constant.50.clone.refs_2_, bf16[2,256,256]{2,1,0:T(8,128)(2,1)} %get-tuple-element.6.refs_3_, f32[256,128]{1,0:T(8,128)} %bitcast.36, ...), custom_call_target="tpu_custom_call" | custom-call | flops 12884901888 | bytes 8388608 | tf_op jit(solution)/shard_map/spectral/pallas_call | solution.py:418
  176.6 51.0 %all-to-all-done.refs_0_ = bf16[16,16,64,128]{3,2,1,0:T(8,128)(2,1)} async-done(((bf16[16,16,64,128]{3,2,1,0:T(8,128)(2,1)}), bf16[16,16,64,128]{3,2,1,0:T(8,128)(2,1)}, u32[]{:S(2)}, u32[]{:S(2)}) %all-to-all-start) | async-done | bytes 4194336 | tf_op jit(solution)/shard_map/all_to_all | solution.py:498
  227.6 4.9 %all-to-all-start.3 = ((bf16[16,16,64,128]{3,2,1,0:T(8,128)(2,1)}), bf16[16,16,64,128]{3,2,1,0:T(8,128)(2,1)}, u32[]{:S(2)}, u32[]{:S(2)}) async-start(bf16[16,16,64,128]{3,2,1,0:T(8,128)(2,1)} %spectral.3), calls=%async_computation.3 | async-start | bytes 8388608 | tf_op jit(solution)/shard_map/all_to_all | solution.py:498
  232.5 35.7 %spectral.2 = bf16[16,16,64,128]{3,2,1,0:T(8,128)(2,1)} custom-call(bf16[16,16,64,128]{3,2,1,0:T(8,128)(2,1)} %all-to-all-done.refs_0_, bf16[1024,1024]{1,0:T(8,128)(2,1)} %constant.49.clone.refs_1_, bf16[1024,1024]{1,0:T(8,128)(2,1)} %constant.50.clone.refs_2_, bf16[2,256,256]{2,1,0:T(8,128)(2,1)} %get-tuple-element.6.refs_3_, f32[256,128]{1,0:T(8,128)} %bitcast.37, ...), custom_call_target="tpu_custom_call" | custom-call | flops 12884901888 | bytes 8388608 | tf_op jit(solution)/shard_map/spectral/pallas_call | solution.py:418
  268.1 56.8 %all-to-all-done.3 = bf16[16,16,64,128]{3,2,1,0:T(8,128)(2,1)} async-done(((bf16[16,16,64,128]{3,2,1,0:T(8,128)(2,1)}), bf16[16,16,64,128]{3,2,1,0:T(8,128)(2,1)}, u32[]{:S(2)}, u32[]{:S(2)}) %all-to-all-start.3) | async-done | bytes 4194336 | tf_op jit(solution)/shard_map/all_to_all | solution.py:498
  324.9 4.9 %all-to-all-start.1 = ((bf16[16,16,64,128]{3,2,1,0:T(8,128)(2,1)}), bf16[16,16,64,128]{3,2,1,0:T(8,128)(2,1)}, u32[]{:S(2)}, u32[]{:S(2)}) async-start(bf16[16,16,64,128]{3,2,1,0:T(8,128)(2,1)} %spectral.2), calls=%async_computation.1 | async-start | bytes 8388608 | tf_op jit(solution)/shard_map/all_to_all | solution.py:498
  329.8 11.4 %inverse.2.refs_0_ = bf16[2,128,64,1024]{3,2,1,0:T(8,128)(2,1)} custom-call(bf16[4,4,16,64,128]{4,3,2,1,0:T(8,128)(2,1)} %bitcast.13.y_ref, bf16[256,1024]{1,0:T(8,128)(2,1)} %constant.48.clone.table_ref), custom_call_target="tpu_custom_call" | custom-call | flops 4294967296 | bytes 25165824 | tf_op jit(solution)/shard_map/inverse/pallas_call | solution.py:443
  341.2 81.1 %all-to-all-done.1 = bf16[16,16,64,128]{3,2,1,0:T(8,128)(2,1)} async-done(((bf16[16,16,64,128]{3,2,1,0:T(8,128)(2,1)}), bf16[16,16,64,128]{3,2,1,0:T(8,128)(2,1)}, u32[]{:S(2)}, u32[]{:S(2)}) %all-to-all-start.1) | async-done | bytes 4194336 | tf_op jit(solution)/shard_map/all_to_all | solution.py:498
  422.3 11.4 %inverse.3 = bf16[2,128,64,1024]{3,2,1,0:T(8,128)(2,1)} custom-call(bf16[4,4,16,64,128]{4,3,2,1,0:T(8,128)(2,1)} %bitcast.11.y_ref, bf16[256,1024]{1,0:T(8,128)(2,1)} %constant.48.clone.table_ref, bf16[2,128,64,1024]{3,2,1,0:T(8,128)(2,1)} %inverse.2.refs_0_), custom_call_target="tpu_custom_call", output_to_operand_aliasing={{}: (2, {})} | custom-call | flops 4294967296 | bytes 25165824 | tf_op jit(solution)/shard_map/inverse/pallas_call | solution.py:443
  (5 shorter events, 0.0 us)
Async XLA Ops:
  6.0 7.5 %collective-permute-start.1 = (f32[2,32,1024]{2,1,0:T(8,128)}, f32[2,32,1024]{2,1,0:T(8,128)S(1)}, u32[]{:S(2)}, u32[]{:S(2)}) collective-permute-start(f32[2,32,1024]{2,1,0:T(8,128)} %stats.3.refs_0_.mine_ref), channel_id=1, source_target_pairs={{0,1},{1,0},{2,3},{3,2},{4,5},{5,4},{6,7},{7,6},{8,9},{9,8},{10,11... | collective-permute-start | bytes 786440 | tf_op jit(solution)/shard_map/ppermute | solution.py:487
  13.3 8.7 %collective-permute-start = (f32[2,32,1024]{2,1,0:T(8,128)}, f32[2,32,1024]{2,1,0:T(8,128)S(1)}, u32[]{:S(2)}, u32[]{:S(2)}) collective-permute-start(f32[2,32,1024]{2,1,0:T(8,128)} %stats.4.mine_ref), channel_id=1, source_target_pairs={{0,1},{1,0},{2,3},{3,2},{4,5},{5,4},{6,7},{7,6},{8,9},{9,8},{10,11... | collective-permute-start | bytes 786440 | tf_op jit(solution)/shard_map/ppermute | solution.py:487
  13.5 0.7 copy-start.2
  21.9 0.7 copy-start.1
  30.4 99.8 %all-to-all-start.2 = ((bf16[16,16,64,128]{3,2,1,0:T(8,128)(2,1)}), bf16[16,16,64,128]{3,2,1,0:T(8,128)(2,1)}, u32[]{:S(2)}, u32[]{:S(2)}) async-start(bf16[16,16,64,128]{3,2,1,0:T(8,128)(2,1)} %bitcast.32), calls=%async_computation.2 | async-start | bytes 8388608 | tf_op jit(solution)/shard_map/all_to_all | solution.py:498
  47.8 13.5 %collective-permute-start.2 = (f32[2,64,1024]{2,1,0:T(8,128)}, f32[2,64,1024]{2,1,0:T(8,128)S(1)}, u32[]{:S(2)}, u32[]{:S(2)}) collective-permute-start(f32[2,64,1024]{2,1,0:T(8,128)} %stats.5.mine_ref), channel_id=1, source_target_pairs={{0,1},{1,0},{2,3},{3,2},{4,5},{5,4},{6,7},{7,6},{8,9},{9,8},{10,11... | collective-permute-start | bytes 1572872 | tf_op jit(solution)/shard_map/ppermute | solution.py:487
  61.2 0.8 copy-start
  130.2 97.4 %all-to-all-start = ((bf16[16,16,64,128]{3,2,1,0:T(8,128)(2,1)}), bf16[16,16,64,128]{3,2,1,0:T(8,128)(2,1)}, u32[]{:S(2)}, u32[]{:S(2)}) async-start(bf16[16,16,64,128]{3,2,1,0:T(8,128)(2,1)} %bitcast.33), calls=%async_computation | async-start | bytes 8388608 | tf_op jit(solution)/shard_map/all_to_all | solution.py:498
  135.1 3.4 copy-start.4
  135.1 3.4 copy-start.5
  135.1 3.4 copy-start.3
  227.6 97.4 %all-to-all-start.3 = ((bf16[16,16,64,128]{3,2,1,0:T(8,128)(2,1)}), bf16[16,16,64,128]{3,2,1,0:T(8,128)(2,1)}, u32[]{:S(2)}, u32[]{:S(2)}) async-start(bf16[16,16,64,128]{3,2,1,0:T(8,128)(2,1)} %spectral.3), calls=%async_computation.3 | async-start | bytes 8388608 | tf_op jit(solution)/shard_map/all_to_all | solution.py:498
  324.9 97.4 %all-to-all-start.1 = ((bf16[16,16,64,128]{3,2,1,0:T(8,128)(2,1)}), bf16[16,16,64,128]{3,2,1,0:T(8,128)(2,1)}, u32[]{:S(2)}, u32[]{:S(2)}) async-start(bf16[16,16,64,128]{3,2,1,0:T(8,128)(2,1)} %spectral.2), calls=%async_computation.1 | async-start | bytes 8388608 | tf_op jit(solution)/shard_map/all_to_all | solution.py:498
